TPU v7x, 32 devices: a whole 2x2x4 slice. The times are simulated.
32 devices in a mesh: face: 4 (over x, core), tile: 8 (over z, y).
Axes of the slice: x: 2, y: 2, z: 4, core: 2. Of those that a mesh axis runs over, the one named last changes fastest.
Arguments:
- predicted_field: bfloat16 [16, 2048, 128], P(None, ('face', 'tile')), may hold values from -6 to 6
- parent_band_holder: int32 [2048, 2], P(('face', 'tile')), may hold values from 0 to 31, all different within a row; in each aligned block of 64 rows (0 to 63, 64 to 127, ...) at most 8 rows name the same one
- parent_band_slot: int32 [2048, 2], P(('face', 'tile')), may hold values from 0 to 63
- neighbour_positions: int32 [4, 2048, 128], P(None, ('face', 'tile')), may hold values from 0 to 255
- unscaled_neighbour_factor: float32 [4, 2048, 128], P(None, ('face', 'tile')), may hold values from 0.05 to 1
- truth_field: float32 [256, 1024], P('tile', 'face'), may hold values from -6 to 6
Outputs:
- predicted_field_slope: float32 [16, 2048, 128], P(None, ('face', 'tile'))
Inputs may be any that keep to these rules, and one draw needn't show every extreme that they name: `parent_band_holder`: the two entries of a row differ. Within the 64 rows of one device no device is named more than 8 times, and some device is named exactly 8 times.
All inputs are finite; a program needn't handle non-finite values.
Results may differ from a plain program's by a relative error of at most 0.0003.
Values may be sent and summed in bfloat16 or wider, within the bound.
A program may use at most 128 MiB of HBM per device.

v0:
```python
import jax
import jax.numpy as jnp
from jax import lax
from jax.sharding import PartitionSpec as P

RANGE = 8


FLOOR = 0.01


def with_halo(cells, sides, width, closed):
    for axis, dim in sides:
        count = lax.axis_size(axis)
        ends = count if closed else count - 1
        head = lax.slice_in_dim(cells, 0, width, axis=dim)
        tail = lax.slice_in_dim(cells, cells.shape[dim] - width, cells.shape[dim], axis=dim)
        cells = jnp.concatenate(
            [
                lax.ppermute(tail, axis, [(i, (i + 1) % count) for i in range(ends)]),
                cells,
                lax.ppermute(head, axis, [((i + 1) % count, i) for i in range(ends)]),
            ],
            axis=dim,
        )
    return cells


def pair_push(first, second, weight, participant_count):
    diff = first[:participant_count] - second[:participant_count]
    square_sum = diff * diff + FLOOR
    inverse_power = square_sum ** (-0.75)
    spread = jnp.mean(square_sum * inverse_power, axis=0)
    observed = first[participant_count] - second[participant_count]
    mismatch = (observed * observed + FLOOR) ** 0.25 - spread
    return weight / participant_count * mismatch * diff * inverse_power


def gather_weighted(values, neighbour_positions, norm_weight):
    participant_count = values.shape[0]
    band_ids = jnp.arange(values.shape[1], dtype=jnp.int32)[:, None]
    summed = jnp.zeros((participant_count,) + neighbour_positions.shape[1:], jnp.float32)
    for point in range(neighbour_positions.shape[0]):
        picked = values[:, band_ids, neighbour_positions[point]]
        summed = summed + picked.astype(jnp.float32) * norm_weight[point][None]
    return summed


def local(
    predicted_field,
    parent_band_holder,
    parent_band_slot,
    neighbour_positions,
    unscaled_neighbour_factor,
    truth_field,
):
    participant_count, resident_band_count, band_pixel_count = predicted_field.shape
    tile_count = lax.axis_size("tile")
    device_count = lax.axis_size(("face", "tile"))
    slot_count = max(2, 4 * resident_band_count // device_count)
    pair_owner = parent_band_holder.reshape(-1)
    owner_hot = (pair_owner[:, None] == jnp.arange(device_count, dtype=jnp.int32)[None, :]).astype(
        jnp.int32
    )
    slot_rank = jnp.sum((jnp.cumsum(owner_hot, axis=0) - owner_hot) * owner_hot, axis=1)
    place = pair_owner * slot_count + slot_rank
    wanted = (
        jnp.zeros((device_count * slot_count,), jnp.int32)
        .at[place]
        .set(parent_band_slot.reshape(-1))
    )
    wanted_band_numbers = lax.all_to_all(
        wanted.reshape(device_count, slot_count),
        ("face", "tile"),
        split_axis=0,
        concat_axis=0,
        tiled=True,
    ).reshape(-1)
    outgoing_bands = jnp.take(predicted_field, wanted_band_numbers, axis=1)
    incoming = lax.all_to_all(
        outgoing_bands.reshape(participant_count, device_count, slot_count, band_pixel_count),
        ("face", "tile"),
        split_axis=1,
        concat_axis=1,
        tiled=True,
    )
    incoming = incoming.reshape(participant_count, device_count * slot_count, band_pixel_count)
    incoming_bands = jnp.take(incoming, place, axis=1).reshape(
        participant_count, resident_band_count, 2 * band_pixel_count
    )
    norm_weight = unscaled_neighbour_factor / jnp.sum(
        unscaled_neighbour_factor, axis=0, keepdims=True
    )
    regridded = gather_weighted(incoming_bands, neighbour_positions, norm_weight)
    row_count = resident_band_count // 2
    col_count = 2 * band_pixel_count
    field = regridded.reshape(participant_count, row_count, col_count)
    stacked = jnp.concatenate([field, truth_field[None]], axis=0)
    tall_ext = with_halo(stacked, (("tile", 1),), RANGE, False)
    wide_ext = with_halo(stacked, (("face", 2),), RANGE, True)
    row_start = lax.axis_index("tile") * row_count - RANGE
    total_rows = row_count * tile_count
    row_ids = row_start + jnp.arange(row_count + 2 * RANGE, dtype=jnp.int32)
    gradient = jnp.zeros((participant_count, row_count, col_count), jnp.float32)
    for offset in range(1, RANGE + 1):
        span = row_count + 2 * RANGE - offset
        pushed = pair_push(
            tall_ext[:, :span], tall_ext[:, offset:], 1.0 / offset, participant_count
        )
        inside = (row_ids[:span] >= 0) & (row_ids[offset:] < total_rows)
        pushed = jnp.where(inside[None, :, None], pushed, 0.0)
        gradient = (
            gradient
            - pushed[:, RANGE : RANGE + row_count]
            + pushed[:, RANGE - offset : RANGE - offset + row_count]
        )
    for offset in range(1, RANGE + 1):
        span = col_count + 2 * RANGE - offset
        pushed = pair_push(
            wide_ext[:, :, :span], wide_ext[:, :, offset:], 1.0 / offset, participant_count
        )
        gradient = (
            gradient
            - pushed[:, :, RANGE : RANGE + col_count]
            + pushed[:, :, RANGE - offset : RANGE - offset + col_count]
        )
    grad_blocks = gradient.reshape(participant_count, resident_band_count, band_pixel_count)
    unused, pullback = jax.vjp(
        lambda values: gather_weighted(values, neighbour_positions, norm_weight),
        jnp.zeros((participant_count, resident_band_count, 2 * band_pixel_count), jnp.float32),
    )
    incoming_slope_parts = pullback(grad_blocks)[0].reshape(
        participant_count, 2 * resident_band_count, band_pixel_count
    )
    slot_grads = (
        jnp.zeros((participant_count, device_count * slot_count, band_pixel_count), jnp.float32)
        .at[:, place]
        .set(incoming_slope_parts)
    )
    returned = lax.all_to_all(
        slot_grads.reshape(participant_count, device_count, slot_count, band_pixel_count),
        ("face", "tile"),
        split_axis=1,
        concat_axis=1,
        tiled=True,
    )
    returned = returned.reshape(participant_count, device_count * slot_count, band_pixel_count)
    predicted_field_slope = (
        jnp.zeros((participant_count, resident_band_count, band_pixel_count), jnp.float32)
        .at[:, wanted_band_numbers]
        .add(returned)
    )
    return predicted_field_slope


def solution(mesh):
    in_specs = (
        P(None, ("face", "tile"), None),
        P(("face", "tile"), None),
        P(("face", "tile"), None),
        P(None, ("face", "tile"), None),
        P(None, ("face", "tile"), None),
        P("tile", "face"),
    )
    out_specs = P(None, ("face", "tile"), None)
    return jax.shard_map(local, mesh=mesh, in_specs=in_specs, out_specs=out_specs, check_vma=False)
```

profile of v0, /device:TPU:0, one launch (start us, length us, event | category | flops | bytes accessed | tf_op | source)
XLA Modules:
  0.0 814.0 jit_solution(17941726410015707000)
XLA Ops:
  0.0 0.8 copy.62
  0.8 0.7 broadcast_multiply_fusion
  2.3 0.8 copy.63
  3.2 1.0 scatter_custom_fusion
  4.2 0.7 all_to_all.12
  4.9 7.3 all-to-all-start
  12.4 0.7 compare_and_fusion.8
  13.1 0.8 or_bitcast_fusion.3
  14.0 0.9 reduce_sum.169
  14.9 0.9 broadcast_divide_fusion
  15.8 0.7 slice_bitcast_fusion.3
  16.6 0.8 and_reduce_fusion
  17.4 0.8 multiply_reduce_fusion
  18.1 1.2 all-to-all-done
  19.8 0.7 reduce.19
  20.6 5.0 gather_fusion
  25.6 1.3 copy_select_fusion
  26.9 4.9 all-to-all-start.1
  32.7 0.6 select_bitcast_fusion.2
  33.3 0.6 select_bitcast_fusion
  34.0 25.4 %all-to-all-done.1 = bf16[16,32,8,128]{3,2,0,1:T(8,128)(2,1)S(1)} async-done(((bf16[16,32,8,128]{3,2,0,1:T(8,128)(2,1)}), bf16[16,32,8,128]{3,2,0,1:T(8,128)(2,1)S(1)}, u32[]{:S(2)}, u32[]{:S(2)}) %all-to-all-start.1) | async-done | bytes 1048608 | tf_op jit(solution)/shard_map/all_to_all | solution.py:80
  59.6 0.7 gather_fusion.1
  60.3 3.1 copy.81
  63.4 7.6 bitcast_select_fusion
  71.1 96.0 %gather_fusion.2 = bf16[8192,16]{1,0:T(8,128)(2,1)S(1)} fusion(bf16[16,64,256]{0,2,1:T(8,128)(2,1)} %bitcast_select_fusion, s32[8192]{0:T(1024)S(1)} %get-tuple-element.29), kind=kCustom, calls=%fused_computation.2 | custom fusion | bytes 589824 | tf_op jit(solution)/shard_map/gather | solution.py:44
  167.1 2.5 convert.4
  169.6 2.9 copy.82
  172.4 96.0 %gather_fusion.3 = bf16[8192,16]{1,0:T(8,128)(2,1)S(1)} fusion(bf16[16,64,256]{0,2,1:T(8,128)(2,1)} %bitcast_select_fusion, s32[8192]{0:T(1024)S(1)} %get-tuple-element.31), kind=kCustom, calls=%fused_computation.3 | custom fusion | bytes 589824 | tf_op jit(solution)/shard_map/gather | solution.py:44
  268.4 2.5 convert.5
  270.9 2.9 copy.83
  273.8 95.9 %gather_fusion.4 = bf16[8192,16]{1,0:T(8,128)(2,1)S(1)} fusion(bf16[16,64,256]{0,2,1:T(8,128)(2,1)} %bitcast_select_fusion, s32[8192]{0:T(1024)S(1)} %get-tuple-element.30), kind=kCustom, calls=%fused_computation.4 | custom fusion | bytes 589824 | tf_op jit(solution)/shard_map/gather | solution.py:44
  369.7 2.5 convert.6
  372.2 3.5 copy.84
  375.8 96.0 %gather_fusion.5 = bf16[8192,16]{1,0:T(8,128)(2,1)S(1)} fusion(bf16[16,64,256]{0,2,1:T(8,128)(2,1)} %bitcast_select_fusion, s32[8192]{0:T(1024)S(1)} %get-tuple-element.32), kind=kCustom, calls=%fused_computation.5 | custom fusion | bytes 589824 | tf_op jit(solution)/shard_map/gather | solution.py:44
  471.8 2.5 convert.7
  474.2 2.9 copy.85
  477.6 1.7 collective-permute-start.3
  479.4 2.2 collective-permute-start
  481.6 1.5 collective-permute-start.1
  483.1 2.4 collective-permute-done.2
  487.4 0.5 fusion.23
  488.0 0.5 fusion.24
  488.5 0.5 fusion.25
  489.0 0.5 fusion.26
  493.9 0.5 fusion.27
  494.6 0.5 power_multiply_fusion
  497.8 1.0 fusion.16
  504.0 2.9 slice_add_fusion
  506.9 1.1 reshape.402
  508.2 2.8 copy.76
  511.1 2.6 copy.75
  513.7 2.6 copy.77
  516.3 2.6 copy.78
  518.9 48.0 %scatter_custom_fusion.4 = f32[16,16384]{0,1:T(8,128)} fusion(s32[8192]{0:T(1024)} %get-tuple-element.39, f32[8192,16]{1,0:T(8,128)} %bitcast.178, f32[]{:T(128)} %constant.34.clone.1), kind=kCustom, calls=%fused_computation.16 | custom fusion | flops 131072 | bytes 1049088
  566.9 48.0 %scatter_custom_fusion.3 = f32[16,16384]{0,1:T(8,128)} fusion(s32[8192]{0:T(1024)} %get-tuple-element.40, f32[8192,16]{1,0:T(8,128)} %bitcast.177, f32[]{:T(128)} %constant.34.clone.1), kind=kCustom, calls=%fused_computation.18 | custom fusion | flops 131072 | bytes 1049088
  614.9 9.8 %add_any.9 = f32[16,16384]{0,1:T(8,128)} add(f32[16,16384]{0,1:T(8,128)} %scatter_custom_fusion.3, f32[16,16384]{0,1:T(8,128)} %scatter_custom_fusion.4) | non-fusion elementwise | flops 262144 | bytes 3145728 | tf_op jit(solution)/shard_map/transpose(jvp())/add_any | solution.py:44
  624.7 48.0 %scatter_custom_fusion.6 = f32[16,16384]{0,1:T(8,128)} fusion(s32[8192]{0:T(1024)} %get-tuple-element.37, f32[8192,16]{1,0:T(8,128)} %bitcast.176, f32[]{:T(128)} %constant.34.clone.1), kind=kCustom, calls=%fused_computation.14 | custom fusion | flops 131072 | bytes 1049088
  672.7 46.6 %scatter_fusion.2 = f32[16,16384]{0,1:T(8,128)} fusion(f32[16,16384]{0,1:T(8,128)} %add_any.9, s32[8192]{0:T(1024)S(1)} %copy-done.7, f32[8192,16]{1,0:T(8,128)} %bitcast.174), kind=kCustom, calls=%fused_computation.11 | custom fusion | flops 131072 | bytes 1605632
  719.3 9.7 %add_any.10 = f32[16,16384]{0,1:T(8,128)} add(f32[16,16384]{0,1:T(8,128)} %scatter_fusion.2, f32[16,16384]{0,1:T(8,128)} %scatter_custom_fusion.6) | non-fusion elementwise | flops 262144 | bytes 3145728 | tf_op jit(solution)/shard_map/transpose(jvp())/add_any | solution.py:44
  729.0 5.1 copy.79
  734.3 4.3 scatter_fusion
  738.7 53.5 %all_to_all.19 = f32[16,32,8,128]{3,0,2,1:T(8,128)} all-to-all(f32[16,32,8,128]{3,0,2,1:T(8,128)S(1)} %bitcast.172), channel_id=1, replica_groups=mesh['face'=4,'tile'=8] {'face','tile'}, dimensions={1} | all-to-all | bytes 4194304 | tf_op jit(solution)/shard_map/all_to_all | solution.py:140
  792.2 20.6 %scatter_fusion.1 = f32[16,64,128]{2,0,1:T(8,128)S(1)} fusion(f32[16,64,128]{2,0,1:T(8,128)S(1)} %broadcast_in_dim.136, s32[256]{0:T(256)S(1)} %bitcast.199, f32[256,16,128]{2,1,0:T(8,128)} %bitcast.173), kind=kCustom, calls=%fused_computation.8 | custom fusion | flops 524288 | bytes 6292480 | tf_op jit(solution)/shard_map/scatter-add | solution.py:151
  812.8 1.0 copy.80
  (103 shorter events, 17.8 us)
Async XLA Ops:
  0.0 20.6 %copy-start = (bf16[16,64,128]{2,1,0:T(8,128)(2,1)S(1)}, bf16[16,64,128]{2,1,0:T(8,128)(2,1)}, u32[]{:S(2)}) copy-start(bf16[16,64,128]{2,1,0:T(8,128)(2,1)} %param.6) | copy-start | bytes 786436
  4.9 14.3 %all-to-all-start = ((s32[32,1,8]{2,1,0:T(1,128)}), s32[32,1,8]{2,1,0:T(1,128)S(1)}, u32[]{:S(2)}, u32[]{:S(2)}) async-start(s32[32,1,8]{2,1,0:T(1,128)} %bitcast.2), calls=%async_computation | async-start | bytes 32768 | tf_op jit(solution)/shard_map/all_to_all | solution.py:72
  26.9 32.5 %all-to-all-start.1 = ((bf16[16,32,8,128]{3,2,0,1:T(8,128)(2,1)}), bf16[16,32,8,128]{3,2,0,1:T(8,128)(2,1)S(1)}, u32[]{:S(2)}, u32[]{:S(2)}) async-start(bf16[16,32,8,128]{3,2,0,1:T(8,128)(2,1)} %copy_select_fusion), calls=%async_computation.1 | async-start | bytes 2097152 | tf_op jit(solution)/shard_map/all_to_all | solution.py:80
  474.2 2.9 copy-start.3
  474.2 3.2 copy-start.2
  477.6 8.0 collective-permute-start.2
  477.6 7.9 collective-permute-start.3
  479.4 15.8 %collective-permute-start = (f32[17,8,256]{2,1,0:T(8,128)S(1)}, f32[17,8,256]{2,1,0:T(8,128)S(1)}, u32[]{:S(2)}, u32[]{:S(2)}) collective-permute-start(f32[17,8,256]{2,1,0:T(8,128)S(1)} %get-tuple-element.13), channel_id=1, source_target_pairs={{0,1},{1,2},{2,3},{3,4},{4,5},{5,6},{6,7},{8,9},{9,10},{10,11},{11... | collective-permute-start | bytes 417800 | tf_op jit(solution)/shard_map/ppermute | solution.py:20
  481.6 13.6 %collective-permute-start.1 = (f32[17,8,256]{2,1,0:T(8,128)S(1)}, f32[17,8,256]{2,1,0:T(8,128)S(1)}, u32[]{:S(2)}, u32[]{:S(2)}) collective-permute-start(f32[17,8,256]{2,1,0:T(8,128)S(1)} %get-tuple-element.14), channel_id=1, source_target_pairs={{1,0},{2,1},{3,2},{4,3},{5,4},{6,5},{7,6},{9,8},{10,9},{11,10},{12... | collective-permute-start | bytes 417800 | tf_op jit(solution)/shard_map/ppermute | solution.py:22
  504.0 4.0 copy-start.4
  504.0 4.0 copy-start.5
  504.0 4.0 copy-start.6
  624.7 48.0 %copy-start.7 = (s32[8192]{0:T(1024)S(1)}, s32[8192]{0:T(1024)}, u32[]{:S(2)}) copy-start(s32[8192]{0:T(1024)} %get-tuple-element.38) | copy-start | bytes 98308
  738.6 75.2 %copy-start.1 = (bf16[16,64,128]{2,1,0:T(8,128)(2,1)S(1)}, bf16[16,64,128]{2,1,0:T(8,128)(2,1)}, u32[]{:S(2)}) copy-start(bf16[16,64,128]{2,1,0:T(8,128)(2,1)} %param.6) | copy-start | bytes 786436
where the time goes:
time: 823 us; the launch traced here: 814 us
  local copies, waits for them, and re-layouts  433 us (53%)
  other arithmetic  280 us (34%)
  blocking collectives  53.5 us (7%)
  waiting for transfers between devices  29 us (4%)
  starting transfers between devices  17.7 us (2%)
    gather x4, local copies, waits for them, and re-layouts, gather_weighted(): picked = values[:, band_ids, neighbour_positions[point]]  384 us
    unnamed x8, other arithmetic  193 us
    all_to_all x1, blocking collectives, local(): lax.all_to_all(slot_grads.reshape(participant_count, device_count, slot_c...  53.5 us
    all_to_all x1, waiting for transfers between devices, local(): lax.all_to_all(outgoing_bands.reshape(participant_count, device_count, sl...  25.4 us
    scatter-add x1, other arithmetic, local(): predicted_field_slope = jnp.zeros((participant_count, resident_band_count...  20.6 us
    add_any x2, other arithmetic, gather_weighted(): picked = values[:, band_ids, neighbour_positions[point]]  19.5 us
  transfers between devices with their start and end apart: 6, of which 3 were waited for; matrix products, arithmetic and copies ran while one was open for 2% of the time, Pallas kernels for 0%

commit v1 on v0

v1 whole, which is shorter than its diff:
```python
import functools

import jax
import jax.numpy as jnp
from jax import lax
from jax.experimental import pallas as pl
from jax.experimental.pallas import tpu as pltpu
from jax.sharding import PartitionSpec as P

RANGE = 8
FLOOR = 0.01
LANES = 128
VMEM = pltpu.VMEM
SMEM = pltpu.SMEM


def spec(space):
    return pl.BlockSpec(memory_space=space)


def root_of(diff):
    return lax.rsqrt(lax.rsqrt(diff * diff + FLOOR))


def lane_pick(values, index):
    return jnp.take_along_axis(values, index, axis=1, mode="promise_in_bounds")


def lane_ids():
    return lax.broadcasted_iota(jnp.int32, (16, LANES), 1)


def regrid_kernel(place, incoming, positions, factors, field, heads, tails, weights):
    total = factors[0] + factors[1] + factors[2] + factors[3]
    for j in range(4):
        weights[j] = factors[j] / total
    members = field.shape[1]
    lane = lax.broadcasted_iota(jnp.int32, (members, LANES), 1)
    per_tile = LANES // RANGE
    for group in range(heads.shape[0]):
        def row_step(r, carry):
            head, tail = carry
            row = group * per_tile + r
            for half in range(2):
                g = 2 * row + half
                first = incoming[place[2 * g]].astype(jnp.float32)
                second = incoming[place[2 * g + 1]].astype(jnp.float32)
                summed = None
                for j in range(4):
                    at = jnp.broadcast_to(positions[j, pl.ds(g, 1), :], (members, LANES))
                    low = at & (LANES - 1)
                    picked = jnp.where(at < LANES, lane_pick(first, low), lane_pick(second, low))
                    term = picked * weights[j, pl.ds(g, 1), :]
                    summed = term if summed is None else summed + term
                field[g] = summed
                mine = (lane >> 3) == r
                if half == 0:
                    head = jnp.where(mine, pltpu.roll(summed, r * RANGE, 1), head)
                else:
                    tail = jnp.where(mine, pltpu.roll(summed, r * RANGE + RANGE, 1), tail)
            return head, tail

        zero = jnp.zeros((members, LANES), jnp.float32)
        head, tail = lax.fori_loop(0, per_tile, row_step, (zero, zero), unroll=2)
        heads[group] = head
        tails[group] = tail


def push_of(first, second, observed_root, scale):
    diff = first - second
    square = diff * diff + FLOOR
    inverse = lax.rsqrt(square)
    root = lax.rsqrt(inverse)
    spread = jnp.sum(root, axis=0, keepdims=True) * (1.0 / first.shape[0])
    mismatch = (observed_root - spread) * scale
    return mismatch * (diff * (root * inverse * inverse))


def score_kernel(
    edge, place, field, above, below, heads, tails, left_tails, right_heads,
    root_tall, root_wide, root_left, root_right, positions, factors,
    slots, ext, grad, weights,
):
    bands, members = field.shape[0], field.shape[1]
    rows = bands // 2
    halo = 2 * RANGE
    total = factors[0] + factors[1] + factors[2] + factors[3]
    for j in range(4):
        weights[j] = factors[j] / total
    ext[pl.ds(0, halo)] = above[...]
    ext[pl.ds(halo, bands)] = field[...]
    ext[pl.ds(halo + bands, halo)] = below[...]
    grad[...] = jnp.zeros_like(grad)

    def tall_step(a, carry):
        for half in range(2):
            mine = ext[2 * a + half]
            own = jnp.zeros_like(mine)
            for k in range(1, RANGE + 1):
                inside = (a >= edge[0]) & (a + k < edge[1])
                scale = jnp.where(inside, 1.0 / (k * members), 0.0)
                other = 2 * (a + k) + half
                push = push_of(
                    mine, ext[other],
                    root_tall[2 * k - 2 + half, pl.ds(a, 1), :], scale,
                )
                own = own - push
                grad[other] = grad[other] + push
            grad[2 * a + half] = grad[2 * a + half] + own
        return carry

    lax.fori_loop(0, rows + RANGE, tall_step, 0)

    lane = lax.broadcasted_iota(jnp.int32, (members, LANES), 1)

    sub = lane & (RANGE - 1)
    per_tile = LANES // RANGE
    for group in range(heads.shape[0]):
        head, tail = heads[group], tails[group]
        left, right = left_tails[group], right_heads[group]
        head_grad = jnp.zeros_like(head)
        tail_grad = jnp.zeros_like(tail)
        for k in range(1, RANGE + 1):
            crossing = sub >= RANGE - k
            scale = 1.0 / (k * members)
            shift = RANGE - k
            moved = pltpu.roll(head, shift, 1) if shift else head
            push = push_of(left, moved, root_left[k - 1, pl.ds(group, 1), :], scale)
            push = jnp.where(crossing, push, 0.0)
            back = pltpu.roll(push, LANES - shift, 1) if shift else push
            head_grad = head_grad + back
            moved = pltpu.roll(right, shift, 1) if shift else right
            push = push_of(tail, moved, root_right[k - 1, pl.ds(group, 1), :], scale)
            tail_grad = tail_grad - jnp.where(crossing, push, 0.0)

        def spread_step(r, carry):
            g = halo + 2 * (group * per_tile + r)
            back = pltpu.roll(head_grad, LANES - r * RANGE, 1)
            grad[g] = grad[g] + jnp.where(lane < RANGE, back, 0.0)
            back = pltpu.roll(tail_grad, LANES - RANGE - r * RANGE, 1)
            grad[g + 1] = grad[g + 1] + jnp.where(lane >= LANES - RANGE, back, 0.0)
            return carry

        lax.fori_loop(0, per_tile, spread_step, 0)

    def wide_step(r, carry):
        g = 2 * r
        west, east = field[g], field[g + 1]
        west_grad, east_grad = grad[halo + g], grad[halo + g + 1]
        for k in range(1, RANGE + 1):
            scale = 1.0 / (k * members)
            within = lane < LANES - k
            after = lane >= k
            west_next = pltpu.roll(west, LANES - k, 1)
            east_next = pltpu.roll(east, LANES - k, 1)
            west_push = push_of(
                west, jnp.where(within, west_next, east_next),
                root_wide[2 * k - 2, pl.ds(r, 1), :], scale,
            )
            east_push = push_of(
                east, east_next, root_wide[2 * k - 1, pl.ds(r, 1), :], scale
            )
            east_push = jnp.where(within, east_push, 0.0)
            west_back = pltpu.roll(west_push, k, 1)
            east_back = pltpu.roll(east_push, k, 1)
            west_grad = west_grad - west_push + jnp.where(after, west_back, 0.0)
            east_grad = east_grad - east_push + jnp.where(after, east_back, west_back)
        for half, value in ((0, west_grad), (1, east_grad)):
            adjoint(g + half, value)
        return carry

    spots = lax.broadcasted_iota(jnp.int32, (2 * LANES, LANES), 0)
    contract = (((1,), (1,)), ((), ()))

    def adjoint(g, value):
        matrix = jnp.zeros((2 * LANES, LANES), jnp.float32)
        for j in range(4):
            at = positions[j, pl.ds(g, 1), :]
            matrix = matrix + jnp.where(spots == at, weights[j, pl.ds(g, 1), :], 0.0)
        high = matrix.astype(jnp.bfloat16)
        low = (matrix - high.astype(jnp.float32)).astype(jnp.bfloat16)
        value_high = value.astype(jnp.bfloat16)
        value_low = (value - value_high.astype(jnp.float32)).astype(jnp.bfloat16)
        slope = (
            lax.dot_general(value_high, high, contract, preferred_element_type=jnp.float32)
            + lax.dot_general(value_low, high, contract, preferred_element_type=jnp.float32)
            + lax.dot_general(value_high, low, contract, preferred_element_type=jnp.float32)
        )
        slots[place[2 * g]] = slope[:, :LANES]
        slots[place[2 * g + 1]] = slope[:, LANES:]

    lax.fori_loop(0, rows, wide_step, 0)


def collect_kernel(wanted, returned, slope, summed):
    bands = slope.shape[1]
    summed[...] = jnp.zeros_like(summed)

    def step(i, carry):
        at = wanted[i]
        summed[at] = summed[at] + returned[i]
        return carry

    lax.fori_loop(0, returned.shape[0], step, 0, unroll=8)
    for g in range(bands):
        slope[:, g, :] = summed[g]


def halves(planes):
    return jnp.stack([p[:, at : at + LANES] for p in planes for at in (0, LANES)])


def shifted(cells, axis, step, closed):
    count = lax.axis_size(axis)
    ends = count if closed else count - 1
    pairs = [(i, (i + 1) % count) for i in range(ends)]
    if step < 0:
        pairs = [(b, a) for a, b in pairs]
    return lax.ppermute(cells, axis, pairs)


def local(
    predicted_field,
    parent_band_holder,
    parent_band_slot,
    neighbour_positions,
    unscaled_neighbour_factor,
    truth_field,
):
    members, bands, pixels = predicted_field.shape
    tile_count = lax.axis_size("tile")
    device_count = lax.axis_size(("face", "tile"))
    slot_count = max(2, 4 * bands // device_count)
    slots_all = device_count * slot_count
    rows, cols = bands // 2, 2 * pixels
    groups = rows * RANGE // LANES

    owner = parent_band_holder.reshape(-1)
    order = jnp.arange(2 * bands, dtype=jnp.int32)
    before = (owner[:, None] == owner[None, :]) & (order[None, :] < order[:, None])
    place = owner * slot_count + jnp.sum(before.astype(jnp.int32), axis=1)
    held = place[None, :] == jnp.arange(slots_all, dtype=jnp.int32)[:, None]
    wanted = bands + jnp.sum(
        jnp.where(held, parent_band_slot.reshape(-1)[None, :] - bands, 0), axis=1
    )
    asked = lax.all_to_all(
        wanted.reshape(device_count, slot_count), ("face", "tile"),
        split_axis=0, concat_axis=0, tiled=True,
    ).reshape(-1)
    strips = jnp.transpose(predicted_field, (1, 0, 2))
    outgoing = jnp.take(strips, jnp.minimum(asked, bands - 1), axis=0)
    incoming = lax.all_to_all(
        outgoing, ("face", "tile"), split_axis=0, concat_axis=0, tiled=True
    )

    truth_above = shifted(truth_field[rows - RANGE :], "tile", 1, False)
    truth_below = shifted(truth_field[:RANGE], "tile", -1, False)
    truth_tall = jnp.concatenate([truth_above, truth_field, truth_below], axis=0)
    root_tall = halves(
        [root_of(truth_tall[: rows + RANGE] - truth_tall[k : k + rows + RANGE]) for k in range(1, RANGE + 1)]
    )
    root_wide = halves(
        [root_of(truth_field - jnp.roll(truth_field, -k, axis=1)) for k in range(1, RANGE + 1)]
    )
    truth_heads = truth_field[:, :RANGE].reshape(groups, LANES)
    truth_tails = truth_field[:, cols - RANGE :].reshape(groups, LANES)
    truth_left = shifted(truth_tails, "face", 1, True)
    truth_right = shifted(truth_heads, "face", -1, True)
    root_left = jnp.stack(
        [root_of(truth_left - jnp.roll(truth_heads, RANGE - k, axis=1)) for k in range(1, RANGE + 1)]
    )
    root_right = jnp.stack(
        [root_of(truth_tails - jnp.roll(truth_right, RANGE - k, axis=1)) for k in range(1, RANGE + 1)]
    )

    f32 = jnp.float32
    side = jax.ShapeDtypeStruct((groups, members, LANES), f32)
    field, heads, tails = pl.pallas_call(
        regrid_kernel,
        out_shape=(jax.ShapeDtypeStruct((bands, members, pixels), f32), side, side),
        in_specs=[spec(SMEM), spec(VMEM), spec(VMEM), spec(VMEM)],
        out_specs=(spec(VMEM), spec(VMEM), spec(VMEM)),
        scratch_shapes=[pltpu.VMEM((4, bands, pixels), f32)],
        compiler_params=pltpu.CompilerParams(vmem_limit_bytes=32 << 20),
        name="regrid",
    )(place, incoming, neighbour_positions, unscaled_neighbour_factor)

    halo = 2 * RANGE
    above = shifted(field[bands - halo :], "tile", 1, False)
    below = shifted(field[:halo], "tile", -1, False)
    left_tails = shifted(tails, "face", 1, True)
    right_heads = shifted(heads, "face", -1, True)
    tile = lax.axis_index("tile")
    edge = jnp.stack(
        [RANGE - tile * rows, RANGE + (tile_count - tile) * rows]
    ).astype(jnp.int32)

    slots = pl.pallas_call(
        score_kernel,
        out_shape=jax.ShapeDtypeStruct((slots_all, members, pixels), f32),
        in_specs=[spec(SMEM), spec(SMEM)] + [spec(VMEM)] * 13,
        out_specs=spec(VMEM),
        scratch_shapes=[
            pltpu.VMEM((bands + 2 * halo, members, pixels), f32),
            pltpu.VMEM((bands + 2 * halo, members, pixels), f32),
            pltpu.VMEM((4, bands, pixels), f32),
        ],
        compiler_params=pltpu.CompilerParams(vmem_limit_bytes=32 << 20),
        name="score",
    )(
        edge, place, field, above, below, heads, tails, left_tails, right_heads,
        root_tall, root_wide, root_left, root_right,
        neighbour_positions, unscaled_neighbour_factor,
    )
    returned = lax.all_to_all(
        slots, ("face", "tile"), split_axis=0, concat_axis=0, tiled=True
    )
    return pl.pallas_call(
        collect_kernel,
        out_shape=jax.ShapeDtypeStruct((members, bands, pixels), f32),
        in_specs=[spec(SMEM), spec(VMEM)],
        out_specs=spec(VMEM),
        scratch_shapes=[pltpu.VMEM((bands + 8, members, pixels), f32)],
        compiler_params=pltpu.CompilerParams(vmem_limit_bytes=32 << 20),
        name="collect",
    )(asked, returned)


def solution(mesh):
    in_specs = (
        P(None, ("face", "tile"), None),
        P(("face", "tile"), None),
        P(("face", "tile"), None),
        P(None, ("face", "tile"), None),
        P(None, ("face", "tile"), None),
        P("tile", "face"),
    )
    out_specs = P(None, ("face", "tile"), None)
    return jax.shard_map(local, mesh=mesh, in_specs=in_specs, out_specs=out_specs, check_vma=False)
```

time: 823 us -> 162 us (0.20)
  local copies, waits for them, and re-layouts: 433 us -> 14.2 us
  other arithmetic: 280 us -> 5.08 us
  Pallas kernels: 0 us -> 29.2 us
  starting transfers between devices: 17.7 us -> 27.1 us
    gather x7 -> x1, local copies, waits for them, and re-layouts: 393 us -> 0.85 us  [local(): outgoing = jnp.take(strips, jnp.minimum(asked, bands - 1), axis=0)]
    unnamed x8 -> x14, other arithmetic: 193 us -> 1.26 us
    pallas_call x0 -> x3, Pallas kernels: none -> 29.2 us  [the longest x1 22.3 us: local(): pl.pallas_call(score_kernel, out_shape=jax.ShapeDtypeStruct((slots_all, m...]
    scatter-add x1 -> x0, other arithmetic: 20.6 us -> none  [local(): predicted_field_slope = jnp.zeros((participant_count, resident_band_count...]
    add_any x2 -> x0, other arithmetic: 19.5 us -> none  [gather_weighted(): picked = values[:, band_ids, neighbour_positions[point]]]
    convert_element_type x4 -> x0, local copies, waits for them, and re-layouts: 12.2 us -> none  [gather_weighted(): summed = summed + picked.astype(jnp.float32) * norm_weight[point][None]]
    mul x11 -> x0, local copies, waits for them, and re-layouts: 11.6 us -> none  [the longest x9 11.4 us: gather_weighted(): summed = summed + picked.astype(jnp.float32) * norm_weight[point][None]]
    select_n x12 -> x2, other arithmetic: 12.8 us -> 1.73 us  [local(): outgoing = jnp.take(strips, jnp.minimum(asked, bands - 1), axis=0)]
  transfers between devices with their start and end apart: 6 -> 10, of which waited for: 3 -> 3; matrix products, arithmetic and copies ran while one was open for 2% -> 12% of each run, Pallas kernels for 0% -> 0%
where the time goes in v1:
time: 162 us; the launch traced here: 161 us
  blocking collectives  53.6 us (33%)
  waiting for transfers between devices  31.2 us (19%)
  Pallas kernels  29.2 us (18%)
  starting transfers between devices  27.1 us (17%)
  local copies, waits for them, and re-layouts  14.2 us (9%)
  other arithmetic  5.08 us (3%)
    all_to_all x1, blocking collectives, local(): lax.all_to_all(slots, ('face', 'tile'), split_axis=0, concat_axis=0, tile...  53.6 us
    all_to_all x1, waiting for transfers between devices, local(): lax.all_to_all(outgoing, ('face', 'tile'), split_axis=0, concat_axis=0, t...  26.9 us
    pallas_call x1, Pallas kernels, local(): pl.pallas_call(score_kernel, out_shape=jax.ShapeDtypeStruct((slots_all, m...  22.3 us
    ppermute x8, starting transfers between devices, shifted(): return lax.ppermute(cells, axis, pairs)  15 us
    slice x22, local copies, waits for them, and re-layouts, local(): jnp.roll(truth_field, -k, axis=1)  6.71 us
    all_to_all x1, starting transfers between devices, local(): lax.all_to_all(wanted.reshape(device_count, slot_count), ('face', 'tile')...  6.23 us
    all_to_all x1, starting transfers between devices, local(): lax.all_to_all(outgoing, ('face', 'tile'), split_axis=0, concat_axis=0, t...  5.83 us
    ppermute x8, waiting for transfers between devices, shifted(): return lax.ppermute(cells, axis, pairs)  4.3 us
  transfers between devices with their start and end apart: 10, of which 3 were waited for; matrix products, arithmetic and copies ran while one was open for 12% of the time, Pallas kernels for 0%

profile of v1, /device:TPU:0, one launch (start us, length us, event | category | flops | bytes accessed | tf_op | source)
XLA Modules:
  0.0 160.9 jit_solution(4054818698826373475)
XLA Ops:
  0.0 0.7 fusion.109
  0.7 1.3 collective-permute-start.5
  2.0 5.5 %collective-permute-start.4 = (f32[8,256]{1,0:T(8,128)S(1)}, f32[8,256]{1,0:T(8,128)S(1)}, u32[]{:S(2)}, u32[]{:S(2)}) collective-permute-start(f32[8,256]{1,0:T(8,128)S(1)} %get-tuple-element.36), channel_id=1, source_target_pairs={{0,1},{1,2},{2,3},{3,4},{4,5},{5,6},{6,7},{8,9},{9,10},{10,11},{11... | collective-permute-start | bytes 24584 | tf_op jit(solution)/shard_map/ppermute | solution.py:219
  7.5 0.7 broadcast_add_fusion.1
  8.2 0.1 copy.20
  8.3 0.1 sub.158
  8.4 0.8 copy.19
  9.2 0.1 reshape.415
  9.3 0.2 convert_reduce_fusion
  9.5 0.1 select_reduce_fusion
  9.7 0.7 add.197
  10.4 6.2 %all-to-all-start = ((s32[32,1,8]{2,1,0:T(1,128)}), s32[32,1,8]{2,1,0:T(1,128)S(1)}, u32[]{:S(2)}, u32[]{:S(2)}) async-start(s32[32,1,8]{2,1,0:T(1,128)} %bitcast), calls=%async_computation | async-start | bytes 32768 | tf_op jit(solution)/shard_map/all_to_all | solution.py:246
  16.6 0.8 fusion.108
  17.4 0.1 reshape.417
  17.5 0.3 collective-permute-start.6
  17.8 0.1 reshape.418
  17.9 1.5 collective-permute-start.7
  19.5 0.8 slice.345
  20.4 0.8 slice.357
  21.2 0.8 slice.341
  22.0 0.8 slice.361
  22.9 0.8 slice.337
  23.7 0.8 slice.333
  24.5 0.8 slice.353
  25.4 0.8 slice.349
  26.2 0.1 reshape.419
  26.8 1.1 copy.25
  28.0 0.1 constant_dynamic-update-slice_fusion.52
  28.2 0.1 constant_dynamic-update-slice_fusion.51
  28.3 0.1 constant_dynamic-update-slice_fusion.50
  28.4 0.1 slice_bitcast_fusion.39
  28.5 0.1 constant_dynamic-update-slice_fusion.49
  28.6 0.1 slice_bitcast_fusion.37
  28.7 0.1 constant_dynamic-update-slice_fusion.48
  28.8 0.1 slice_bitcast_fusion.35
  28.9 0.1 constant_dynamic-update-slice_fusion.47
  28.9 0.1 slice_bitcast_fusion.33
  29.0 0.1 constant_dynamic-update-slice_fusion.46
  29.1 0.1 constant_dynamic-update-slice_fusion.44
  29.2 0.1 constant_dynamic-update-slice_fusion.43
  29.3 0.1 constant_dynamic-update-slice_fusion.42
  29.4 0.1 constant_dynamic-update-slice_fusion.41
  29.5 0.1 constant_dynamic-update-slice_fusion.40
  29.6 0.1 constant_dynamic-update-slice_fusion.39
  29.7 0.1 constant_dynamic-update-slice_fusion.38
  29.8 0.5 broadcast.167
  30.4 0.7 minimum_reduce_fusion
  31.1 0.1 min.26
  31.2 0.1 reshape.416.wanted
  31.3 0.8 gather_fusion
  32.3 1.7 %broadcast_select_fusion = bf16[256,16,128]{2,1,0:T(8,128)(2,1)} fusion(bf16[256,16,128]{2,1,0:T(8,128)(2,1)S(1)} %gather_fusion, pred[256]{0:T(512)(128)(4,1)S(1)} %compare_and_fusion), kind=kLoop, calls=%fused_computation.1 | loop fusion | flops 524288 | bytes 2097408 | tf_op jit(solution)/shard_map/jit(_take)/select_n | solution.py:251
  34.0 5.8 %all-to-all-start.1 = ((bf16[256,16,128]{2,1,0:T(8,128)(2,1)}), bf16[256,16,128]{2,1,0:T(8,128)(2,1)S(1)}, u32[]{:S(2)}, u32[]{:S(2)}) async-start(bf16[256,16,128]{2,1,0:T(8,128)(2,1)} %broadcast_select_fusion), calls=%async_computation.1 | async-start | bytes 2097152 | tf_op jit(solution)/shard_map/all_to_all | solution.py:252
  39.9 0.1 fusion.64
  40.3 0.1 fusion.4
  40.6 26.9 %all-to-all-done.1.incoming = bf16[256,16,128]{2,1,0:T(8,128)(2,1)S(1)} async-done(((bf16[256,16,128]{2,1,0:T(8,128)(2,1)}), bf16[256,16,128]{2,1,0:T(8,128)(2,1)S(1)}, u32[]{:S(2)}, u32[]{:S(2)}) %all-to-all-start.1) | async-done | bytes 1048608 | tf_op jit(solution)/shard_map/all_to_all | solution.py:252
  67.4 4.0 %regrid.1 = (f32[64,16,128]{2,1,0:T(8,128)S(1)}, f32[2,16,128]{2,1,0:T(8,128)S(1)}, f32[2,16,128]{2,1,0:T(8,128)S(1)}) custom-call(s32[128]{0:T(128)S(1)} %multiply_add_fusion.place, bf16[256,16,128]{2,1,0:T(8,128)(2,1)S(1)} %all-to-all-done.1.incoming, s32[4,64,128]{2,1,0:T(8,128)S(1)} %copy-done, f32[4,64,128]{2,1,0:T(8,128)S(1)} %copy-done.1), custom_call_target="tpu_custom_call" | custom-call | tf_op jit(solution)/shard_map/regrid/pallas_call | solution.py:278
  71.4 0.5 collective-permute-start.3
  71.9 1.3 collective-permute-start.1
  73.2 4.6 %collective-permute-start = (f32[16,16,128]{2,1,0:T(8,128)S(1)}, f32[16,16,128]{2,1,0:T(8,128)S(1)}, u32[]{:S(2)}, u32[]{:S(2)}) collective-permute-start(f32[16,16,128]{2,1,0:T(8,128)S(1)} %get-tuple-element.14), channel_id=1, source_target_pairs={{0,1},{1,2},{2,3},{3,4},{4,5},{5,6},{6,7},{8,9},{9,10},{10,11},{11... | collective-permute-start | bytes 393224 | tf_op jit(solution)/shard_map/ppermute | solution.py:219
  77.8 2.3 %collective-permute-done.1.below = f32[16,16,128]{2,1,0:T(8,128)S(1)} collective-permute-done((f32[16,16,128]{2,1,0:T(8,128)S(1)}, f32[16,16,128]{2,1,0:T(8,128)S(1)}, u32[]{:S(2)}, u32[]{:S(2)}) %collective-permute-start.1) | collective-permute-done | bytes 131104 | tf_op jit(solution)/shard_map/ppermute | solution.py:219
  80.1 2.0 %collective-permute-done.above = f32[16,16,128]{2,1,0:T(8,128)S(1)} collective-permute-done((f32[16,16,128]{2,1,0:T(8,128)S(1)}, f32[16,16,128]{2,1,0:T(8,128)S(1)}, u32[]{:S(2)}, u32[]{:S(2)}) %collective-permute-start) | collective-permute-done | bytes 131104 | tf_op jit(solution)/shard_map/ppermute | solution.py:219
  82.1 22.3 %score.1 = f32[256,16,128]{2,1,0:T(8,128)S(1)} custom-call(s32[2]{0:T(128)S(1)} %pad_add_fusion.edge, s32[128]{0:T(128)S(1)} %multiply_add_fusion.place, f32[64,16,128]{2,1,0:T(8,128)S(1)} %get-tuple-element.8.field, f32[16,16,128]{2,1,0:T(8,128)S(1)} %collective-permute-done.above, f32[16,16,128]{2,1,0:T(8,128)S(1)} %collective-permute-done.1.below, ...), custom_call_target="tpu_custom_call" | custom-call | tf_op jit(solution)/shard_map/score/pallas_call | solution.py:298
  104.4 53.6 %all_to_all.16.returned = f32[256,16,128]{2,1,0:T(8,128)S(1)} all-to-all(f32[256,16,128]{2,1,0:T(8,128)S(1)} %score.1), channel_id=1, replica_groups=mesh['face'=4,'tile'=8] {'face','tile'}, dimensions={0} | all-to-all | bytes 4194304 | tf_op jit(solution)/shard_map/all_to_all | solution.py:315
  158.0 2.9 %collect.1 = f32[16,64,128]{2,1,0:T(8,128)} custom-call(s32[256]{0:T(256)S(1)} %reshape.416.wanted, f32[256,16,128]{2,1,0:T(8,128)S(1)} %all_to_all.16.returned), custom_call_target="tpu_custom_call" | custom-call | tf_op jit(solution)/shard_map/collect/pallas_call | solution.py:318
  (88 shorter events, 1.1 us)
Async XLA Ops:
  0.7 39.5 %collective-permute-start.5 = (f32[8,256]{1,0:T(8,128)S(1)}, f32[8,256]{1,0:T(8,128)S(1)}, u32[]{:S(2)}, u32[]{:S(2)}) collective-permute-start(f32[8,256]{1,0:T(8,128)S(1)} %get-tuple-element.35), channel_id=1, source_target_pairs={{1,0},{2,1},{3,2},{4,3},{5,4},{6,5},{7,6},{9,8},{10,9},{11,10},{12... | collective-permute-start | bytes 24584 | tf_op jit(solution)/shard_map/ppermute | solution.py:219
  2.0 37.8 %collective-permute-start.4 = (f32[8,256]{1,0:T(8,128)S(1)}, f32[8,256]{1,0:T(8,128)S(1)}, u32[]{:S(2)}, u32[]{:S(2)}) collective-permute-start(f32[8,256]{1,0:T(8,128)S(1)} %get-tuple-element.36), channel_id=1, source_target_pairs={{0,1},{1,2},{2,3},{3,4},{4,5},{5,6},{6,7},{8,9},{9,10},{10,11},{11... | collective-permute-start | bytes 24584 | tf_op jit(solution)/shard_map/ppermute | solution.py:219
  10.4 19.5 %all-to-all-start = ((s32[32,1,8]{2,1,0:T(1,128)}), s32[32,1,8]{2,1,0:T(1,128)S(1)}, u32[]{:S(2)}, u32[]{:S(2)}) async-start(s32[32,1,8]{2,1,0:T(1,128)} %bitcast), calls=%async_computation | async-start | bytes 32768 | tf_op jit(solution)/shard_map/all_to_all | solution.py:246
  17.5 11.6 %collective-permute-start.6 = (f32[2,128]{1,0:T(2,128)S(1)}, f32[2,128]{1,0:T(2,128)S(1)}, u32[]{:S(2)}, u32[]{:S(2)}) collective-permute-start(f32[2,128]{1,0:T(2,128)S(1)} %reshape.417), channel_id=1, source_target_pairs={{0,8},{8,16},{16,24},{24,0},{1,9},{9,17},{17,25},{25,1},{2,10},{10... | collective-permute-start | bytes 3080 | tf_op jit(solution)/shard_map/ppermute | solution.py:219
  17.9 10.0 %collective-permute-start.7 = (f32[2,128]{1,0:T(2,128)S(1)}, f32[2,128]{1,0:T(2,128)S(1)}, u32[]{:S(2)}, u32[]{:S(2)}) collective-permute-start(f32[2,128]{1,0:T(2,128)S(1)} %reshape.418), channel_id=1, source_target_pairs={{8,0},{16,8},{24,16},{0,24},{9,1},{17,9},{25,17},{1,25},{10,2},{18... | collective-permute-start | bytes 3080 | tf_op jit(solution)/shard_map/ppermute | solution.py:219
  32.2 7.7 %copy-start.2 = (f32[32,256]{1,0:T(8,128)S(1)}, f32[32,256]{1,0:T(8,128)}, u32[]{:S(2)}) copy-start(f32[32,256]{1,0:T(8,128)} %param.11) | copy-start | bytes 98308
  32.2 7.7 %slice-start = ((f32[32,256]{1,0:T(8,128)}), f32[32,7]{1,0:T(8,128)S(1)}, s32[]{:S(2)}) async-start(f32[32,256]{1,0:T(8,128)} %param.11), calls=%async_computation.3 | async-start | bytes 32768 | tf_op jit(solution)/shard_map/jit(_roll_static)/slice | solution.py:263
  32.2 7.7 %slice-start.1 = ((f32[32,256]{1,0:T(8,128)}), f32[32,4]{1,0:T(8,128)S(1)}, s32[]{:S(2)}) async-start(f32[32,256]{1,0:T(8,128)} %param.11), calls=%async_computation.4 | async-start | bytes 32768 | tf_op jit(solution)/shard_map/jit(_roll_static)/slice | solution.py:263
  32.2 7.7 %slice-start.2 = ((f32[32,256]{1,0:T(8,128)}), f32[32,3]{1,0:T(8,128)S(1)}, s32[]{:S(2)}) async-start(f32[32,256]{1,0:T(8,128)} %param.11), calls=%async_computation.5 | async-start | bytes 32768 | tf_op jit(solution)/shard_map/jit(_roll_static)/slice | solution.py:263
  32.2 7.7 %slice-start.3 = ((f32[32,256]{1,0:T(8,128)}), f32[32,2]{1,0:T(8,128)S(1)}, s32[]{:S(2)}) async-start(f32[32,256]{1,0:T(8,128)} %param.11), calls=%async_computation.6 | async-start | bytes 32768 | tf_op jit(solution)/shard_map/jit(_roll_static)/slice | solution.py:263
  32.2 7.7 %slice-start.4 = ((f32[32,256]{1,0:T(8,128)}), f32[32,6]{1,0:T(8,128)S(1)}, s32[]{:S(2)}) async-start(f32[32,256]{1,0:T(8,128)} %param.11), calls=%async_computation.7 | async-start | bytes 32768 | tf_op jit(solution)/shard_map/jit(_roll_static)/slice | solution.py:263
  32.2 7.7 %slice-start.5 = ((f32[32,256]{1,0:T(8,128)}), f32[32,1]{1,0:T(8,128)S(1)}, s32[]{:S(2)}) async-start(f32[32,256]{1,0:T(8,128)} %param.11), calls=%async_computation.8 | async-start | bytes 32768 | tf_op jit(solution)/shard_map/jit(_roll_static)/slice | solution.py:263
  32.3 7.7 %slice-start.6 = ((f32[32,256]{1,0:T(8,128)}), f32[32,5]{1,0:T(8,128)S(1)}, s32[]{:S(2)}) async-start(f32[32,256]{1,0:T(8,128)} %param.11), calls=%async_computation.9 | async-start | bytes 32768 | tf_op jit(solution)/shard_map/jit(_roll_static)/slice | solution.py:263
  34.0 33.4 %copy-start = (s32[4,64,128]{2,1,0:T(8,128)S(1)}, s32[4,64,128]{2,1,0:T(8,128)}, u32[]{:S(2)}) copy-start(s32[4,64,128]{2,1,0:T(8,128)} %positions.3) | copy-start | bytes 393220
  34.0 33.4 %copy-start.1 = (f32[4,64,128]{2,1,0:T(8,128)S(1)}, f32[4,64,128]{2,1,0:T(8,128)}, u32[]{:S(2)}) copy-start(f32[4,64,128]{2,1,0:T(8,128)} %factors.3) | copy-start | bytes 393220
  34.0 33.4 %all-to-all-start.1 = ((bf16[256,16,128]{2,1,0:T(8,128)(2,1)}), bf16[256,16,128]{2,1,0:T(8,128)(2,1)S(1)}, u32[]{:S(2)}, u32[]{:S(2)}) async-start(bf16[256,16,128]{2,1,0:T(8,128)(2,1)} %broadcast_select_fusion), calls=%async_computation.1 | async-start | bytes 2097152 | tf_op jit(solution)/shard_map/all_to_all | solution.py:252
  71.4 6.4 %collective-permute-start.3 = (f32[2,16,128]{2,1,0:T(8,128)S(1)}, f32[2,16,128]{2,1,0:T(8,128)S(1)}, u32[]{:S(2)}, u32[]{:S(2)}) collective-permute-start(f32[2,16,128]{2,1,0:T(8,128)S(1)} %get-tuple-element.9.heads), channel_id=1, source_target_pairs={{8,0},{16,8},{24,16},{0,24},{9,1},{17,9},{25,17},{1,25},{10,2},{18... | collective-permute-start | bytes 49160 | tf_op jit(solution)/shard_map/ppermute | solution.py:219
  71.9 6.0 %collective-permute-start.2 = (f32[2,16,128]{2,1,0:T(8,128)S(1)}, f32[2,16,128]{2,1,0:T(8,128)S(1)}, u32[]{:S(2)}, u32[]{:S(2)}) collective-permute-start(f32[2,16,128]{2,1,0:T(8,128)S(1)} %get-tuple-element.10.tails), channel_id=1, source_target_pairs={{0,8},{8,16},{16,24},{24,0},{1,9},{9,17},{17,25},{25,1},{2,10},{10... | collective-permute-start | bytes 49160 | tf_op jit(solution)/shard_map/ppermute | solution.py:219
  71.9 8.2 %collective-permute-start.1 = (f32[16,16,128]{2,1,0:T(8,128)S(1)}, f32[16,16,128]{2,1,0:T(8,128)S(1)}, u32[]{:S(2)}, u32[]{:S(2)}) collective-permute-start(f32[16,16,128]{2,1,0:T(8,128)S(1)} %get-tuple-element.13), channel_id=1, source_target_pairs={{1,0},{2,1},{3,2},{4,3},{5,4},{6,5},{7,6},{9,8},{10,9},{11,10},{12... | collective-permute-start | bytes 393224 | tf_op jit(solution)/shard_map/ppermute | solution.py:219
  73.2 8.9 %collective-permute-start = (f32[16,16,128]{2,1,0:T(8,128)S(1)}, f32[16,16,128]{2,1,0:T(8,128)S(1)}, u32[]{:S(2)}, u32[]{:S(2)}) collective-permute-start(f32[16,16,128]{2,1,0:T(8,128)S(1)} %get-tuple-element.14), channel_id=1, source_target_pairs={{0,1},{1,2},{2,3},{3,4},{4,5},{5,6},{6,7},{8,9},{9,10},{10,11},{11... | collective-permute-start | bytes 393224 | tf_op jit(solution)/shard_map/ppermute | solution.py:219

commit v2 on v1

--- a/solution.py
+++ b/solution.py
@@ -10,6 +10,8 @@
 RANGE = 8
 FLOOR = 0.01
 LANES = 128
+STEPS = 32000.0
+SHARE = 16384.0
 VMEM = pltpu.VMEM
 SMEM = pltpu.SMEM
 
@@ -76,17 +78,64 @@
     return mismatch * (diff * (root * inverse * inverse))
 
 
+def prepare_kernel(
+    truth, above, below, heads, tails, left, right, positions, factors,
+    root_tall, root_wide, root_left, root_right, high, low, tall, weights,
+):
+    rows = truth.shape[0]
+    tall[pl.ds(0, RANGE)] = above[...]
+    tall[pl.ds(RANGE, rows)] = truth[...]
+    tall[pl.ds(RANGE + rows, RANGE)] = below[...]
+    span = rows + RANGE
+    for k in range(1, RANGE + 1):
+        root = root_of(tall[pl.ds(0, span), :] - tall[pl.ds(k, span), :])
+        root_tall[2 * k - 2] = root[:, :LANES]
+        root_tall[2 * k - 1] = root[:, LANES:]
+        west, east = truth[:, :LANES], truth[:, LANES:]
+        lane = lax.broadcasted_iota(jnp.int32, west.shape, 1)
+        west_next = pltpu.roll(west, LANES - k, 1)
+        east_next = pltpu.roll(east, LANES - k, 1)
+        root_wide[2 * k - 2] = root_of(west - jnp.where(lane < LANES - k, west_next, east_next))
+        root_wide[2 * k - 1] = root_of(east - east_next)
+        shift = RANGE - k
+        near = heads[...]
+        far = right[...]
+        if shift:
+            near = jnp.concatenate([near[:, LANES - shift :], near[:, : LANES - shift]], axis=1)
+            far = jnp.concatenate([far[:, LANES - shift :], far[:, : LANES - shift]], axis=1)
+        root_left[k - 1] = root_of(left[...] - near)
+        root_right[k - 1] = root_of(tails[...] - far)
+    total = factors[0] + factors[1] + factors[2] + factors[3]
+    for j in range(4):
+        weights[j] = factors[j] / total
+    spots = lax.broadcasted_iota(jnp.int32, (2 * LANES, LANES), 0)
+
+    def step(g, carry):
+        matrix = jnp.zeros((2 * LANES, LANES), jnp.float32)
+        for j in range(4):
+            at = positions[j, pl.ds(g, 1), :]
+            matrix = matrix + jnp.where(spots == at, weights[j, pl.ds(g, 1), :], 0.0)
+        matrix = matrix.T
+        top = matrix.astype(jnp.bfloat16)
+        high[g] = top
+        low[g] = (matrix - top.astype(jnp.float32)).astype(jnp.bfloat16)
+        return carry
+
+    lax.fori_loop(0, high.shape[0], step, 0)
+
+
 def score_kernel(
     edge, place, field, above, below, heads, tails, left_tails, right_heads,
-    root_tall, root_wide, root_left, root_right, positions, factors,
-    slots, ext, grad, weights,
+    root_tall, root_wide, root_left, root_right, high_far, low_far,
+    slots, ext, grad, scales, high, low, arrived,
 ):
     bands, members = field.shape[0], field.shape[1]
     rows = bands // 2
     halo = 2 * RANGE
-    total = factors[0] + factors[1] + factors[2] + factors[3]
-    for j in range(4):
-        weights[j] = factors[j] / total
+    fetch_high = pltpu.make_async_copy(high_far, high, arrived.at[0])
+    fetch_low = pltpu.make_async_copy(low_far, low, arrived.at[1])
+    fetch_high.start()
+    fetch_low.start()
     ext[pl.ds(0, halo)] = above[...]
     ext[pl.ds(halo, bands)] = field[...]
     ext[pl.ds(halo + bands, halo)] = below[...]
@@ -169,39 +218,56 @@
             adjoint(g + half, value)
         return carry
 
-    spots = lax.broadcasted_iota(jnp.int32, (2 * LANES, LANES), 0)
-    contract = (((1,), (1,)), ((), ()))
+    slot_count = slots.shape[1] - 1
 
     def adjoint(g, value):
-        matrix = jnp.zeros((2 * LANES, LANES), jnp.float32)
-        for j in range(4):
-            at = positions[j, pl.ds(g, 1), :]
-            matrix = matrix + jnp.where(spots == at, weights[j, pl.ds(g, 1), :], 0.0)
-        high = matrix.astype(jnp.bfloat16)
-        low = (matrix - high.astype(jnp.float32)).astype(jnp.bfloat16)
         value_high = value.astype(jnp.bfloat16)
         value_low = (value - value_high.astype(jnp.float32)).astype(jnp.bfloat16)
+        both = jnp.concatenate([value_high, value_low], axis=0)
+        main = jnp.dot(both, high[g], preferred_element_type=jnp.float32)
         slope = (
-            lax.dot_general(value_high, high, contract, preferred_element_type=jnp.float32)
-            + lax.dot_general(value_low, high, contract, preferred_element_type=jnp.float32)
-            + lax.dot_general(value_high, low, contract, preferred_element_type=jnp.float32)
+            main[:members] + main[members:]
+            + jnp.dot(value_high, low[g], preferred_element_type=jnp.float32)
         )
-        slots[place[2 * g]] = slope[:, :LANES]
-        slots[place[2 * g + 1]] = slope[:, LANES:]
-
+        for half in range(2):
+            part = slope[:, half * LANES : (half + 1) * LANES]
+            largest = jnp.max(jnp.abs(part), axis=1, keepdims=True)
+            step = jnp.maximum(largest, 1e-30) * (1.0 / STEPS)
+            code = jnp.round(part * (1.0 / step)).astype(jnp.int32)
+            at = place[2 * g + half]
+            holder = at // slot_count
+            rank = at - holder * slot_count
+            slots[holder, rank] = code.astype(jnp.int16)
+            power = jnp.ceil(jnp.log2(step))
+            share = jnp.round(step * jnp.exp2(-power) * SHARE)
+            old = scales[holder]
+            old = jnp.where(lane == rank, power.astype(jnp.int32), old)
+            scales[holder] = jnp.where(lane == rank + LANES // 2, share.astype(jnp.int32), old)
+
+    fetch_high.wait()
+    fetch_low.wait()
     lax.fori_loop(0, rows, wide_step, 0)
+    for holder in range(slots.shape[0]):
+        slots[holder, slot_count] = scales[holder].astype(jnp.int16)
 
 
 def collect_kernel(wanted, returned, slope, summed):
     bands = slope.shape[1]
     summed[...] = jnp.zeros_like(summed)
 
-    def step(i, carry):
-        at = wanted[i]
-        summed[at] = summed[at] + returned[i]
+    slot_count = returned.shape[1] - 1
+
+    def step(d, carry):
+        scale = returned[d, slot_count].astype(jnp.int32).astype(jnp.float32)
+        share = pltpu.roll(scale, LANES // 2, 1) * (1.0 / SHARE)
+        step_of = share * jnp.exp2(scale)
+        for k in range(slot_count):
+            at = wanted[d * slot_count + k]
+            code = returned[d, k].astype(jnp.int32).astype(jnp.float32)
+            summed[at] = summed[at] + code * step_of[:, k : k + 1]
         return carry
 
-    lax.fori_loop(0, returned.shape[0], step, 0, unroll=8)
+    lax.fori_loop(0, returned.shape[0], step, 0)
     for g in range(bands):
         slope[:, g, :] = summed[g]
 
@@ -253,27 +319,39 @@
         outgoing, ("face", "tile"), split_axis=0, concat_axis=0, tiled=True
     )
 
+    truth_field, asked_late = lax.optimization_barrier((truth_field, asked))
     truth_above = shifted(truth_field[rows - RANGE :], "tile", 1, False)
     truth_below = shifted(truth_field[:RANGE], "tile", -1, False)
-    truth_tall = jnp.concatenate([truth_above, truth_field, truth_below], axis=0)
-    root_tall = halves(
-        [root_of(truth_tall[: rows + RANGE] - truth_tall[k : k + rows + RANGE]) for k in range(1, RANGE + 1)]
-    )
-    root_wide = halves(
-        [root_of(truth_field - jnp.roll(truth_field, -k, axis=1)) for k in range(1, RANGE + 1)]
-    )
     truth_heads = truth_field[:, :RANGE].reshape(groups, LANES)
     truth_tails = truth_field[:, cols - RANGE :].reshape(groups, LANES)
     truth_left = shifted(truth_tails, "face", 1, True)
     truth_right = shifted(truth_heads, "face", -1, True)
-    root_left = jnp.stack(
-        [root_of(truth_left - jnp.roll(truth_heads, RANGE - k, axis=1)) for k in range(1, RANGE + 1)]
-    )
-    root_right = jnp.stack(
-        [root_of(truth_tails - jnp.roll(truth_right, RANGE - k, axis=1)) for k in range(1, RANGE + 1)]
-    )
-
     f32 = jnp.float32
+    matrices = jax.ShapeDtypeStruct((bands, pixels, 2 * pixels), jnp.bfloat16)
+    root_tall, root_wide, root_left, root_right, high, low = pl.pallas_call(
+        prepare_kernel,
+        out_shape=(
+            jax.ShapeDtypeStruct((2 * RANGE, rows + RANGE, LANES), f32),
+            jax.ShapeDtypeStruct((2 * RANGE, rows, LANES), f32),
+            jax.ShapeDtypeStruct((RANGE, groups, LANES), f32),
+            jax.ShapeDtypeStruct((RANGE, groups, LANES), f32),
+            matrices,
+            matrices,
+        ),
+        in_specs=[spec(VMEM)] * 9,
+        out_specs=(spec(VMEM),) * 6,
+        scratch_shapes=[
+            pltpu.VMEM((rows + 2 * RANGE, cols), f32),
+            pltpu.VMEM((4, bands, pixels), f32),
+        ],
+        compiler_params=pltpu.CompilerParams(vmem_limit_bytes=40 << 20),
+        cost_estimate=pl.CostEstimate(flops=10**9, bytes_accessed=16 << 20, transcendentals=0),
+        name="prepare",
+    )(
+        truth_field, truth_above, truth_below, truth_heads, truth_tails, truth_left, truth_right,
+        neighbour_positions, unscaled_neighbour_factor,
+    )
+
     side = jax.ShapeDtypeStruct((groups, members, LANES), f32)
     field, heads, tails = pl.pallas_call(
         regrid_kernel,
@@ -297,20 +375,22 @@
 
     slots = pl.pallas_call(
         score_kernel,
-        out_shape=jax.ShapeDtypeStruct((slots_all, members, pixels), f32),
-        in_specs=[spec(SMEM), spec(SMEM)] + [spec(VMEM)] * 13,
+        out_shape=jax.ShapeDtypeStruct((device_count, slot_count + 1, members, pixels), jnp.int16),
+        in_specs=[spec(SMEM), spec(SMEM)] + [spec(VMEM)] * 11 + [spec(pl.ANY)] * 2,
         out_specs=spec(VMEM),
         scratch_shapes=[
             pltpu.VMEM((bands + 2 * halo, members, pixels), f32),
             pltpu.VMEM((bands + 2 * halo, members, pixels), f32),
-            pltpu.VMEM((4, bands, pixels), f32),
+            pltpu.VMEM((device_count, members, pixels), jnp.int32),
+            pltpu.VMEM((bands, pixels, 2 * pixels), jnp.bfloat16),
+            pltpu.VMEM((bands, pixels, 2 * pixels), jnp.bfloat16),
+            pltpu.SemaphoreType.DMA((2,)),
         ],
-        compiler_params=pltpu.CompilerParams(vmem_limit_bytes=32 << 20),
+        compiler_params=pltpu.CompilerParams(vmem_limit_bytes=40 << 20),
         name="score",
     )(
         edge, place, field, above, below, heads, tails, left_tails, right_heads,
-        root_tall, root_wide, root_left, root_right,
-        neighbour_positions, unscaled_neighbour_factor,
+        root_tall, root_wide, root_left, root_right, high, low,
     )
     returned = lax.all_to_all(
         slots, ("face", "tile"), split_axis=0, concat_axis=0, tiled=True

time: 162 us -> 134 us (0.83)
  blocking collectives: 53.6 us -> 33 us
  Pallas kernels: 29.2 us -> 42.4 us
  local copies, waits for them, and re-layouts: 14.2 us -> 4.78 us
  waiting for transfers between devices: 31.2 us -> 26.5 us
  starting transfers between devices: 27.1 us -> 23 us
    all_to_all x1, blocking collectives: 53.6 us -> 33 us  [local(): lax.all_to_all(slots, ('face', 'tile'), split_axis=0, concat_axis=0, tile...]
    pallas_call x1 -> x2, Pallas kernels: 22.3 us -> 30.8 us  [the longest x1 22.1 us: local(): pl.pallas_call(score_kernel, out_shape=jax.ShapeDtypeStruct((device_count...]
    slice x29 -> x0, local copies, waits for them, and re-layouts: 7.21 us -> none  [the longest x22 6.71 us: local(): jnp.roll(truth_field, -k, axis=1)]
    all_to_all x1, waiting for transfers between devices: 26.9 us -> 20.6 us  [local(): lax.all_to_all(outgoing, ('face', 'tile'), split_axis=0, concat_axis=0, t...]
    all_to_all x1, waiting for transfers between devices: 0.01 us -> 5.91 us  [local(): lax.all_to_all(wanted.reshape(device_count, slot_count), ('face', 'tile')...]
    pallas_call x1, Pallas kernels: 2.86 us -> 7.71 us  [local(): pl.pallas_call(collect_kernel, out_shape=jax.ShapeDtypeStruct((members, b...]
    ppermute x8, waiting for transfers between devices: 4.3 us -> 0.02 us  [shifted(): return lax.ppermute(cells, axis, pairs)]
    all_to_all x1, starting transfers between devices: 5.83 us -> 2.64 us  [local(): lax.all_to_all(outgoing, ('face', 'tile'), split_axis=0, concat_axis=0, t...]
  transfers between devices with their start and end apart: 10 -> 10, of which waited for: 3 -> 2; matrix products, arithmetic and copies ran while one was open for 12% -> 1% of each run, Pallas kernels for 0% -> 9%
where the time goes in v2:
time: 134 us; the launch traced here: 133 us
  Pallas kernels  42.4 us (32%)
  blocking collectives  33 us (25%)
  waiting for transfers between devices  26.5 us (20%)
  starting transfers between devices  23 us (17%)
  local copies, waits for them, and re-layouts  4.78 us (4%)
  other arithmetic  3.57 us (3%)
    all_to_all x1, blocking collectives, local(): lax.all_to_all(slots, ('face', 'tile'), split_axis=0, concat_axis=0, tile...  33 us
    pallas_call x1, Pallas kernels, local(): pl.pallas_call(score_kernel, out_shape=jax.ShapeDtypeStruct((device_count...  22.1 us
    all_to_all x1, waiting for transfers between devices, local(): lax.all_to_all(outgoing, ('face', 'tile'), split_axis=0, concat_axis=0, t...  20.6 us
    ppermute x8, starting transfers between devices, shifted(): return lax.ppermute(cells, axis, pairs)  13.1 us
    pallas_call x1, Pallas kernels, local(): pl.pallas_call(prepare_kernel, out_shape=(jax.ShapeDtypeStruct((2 * RANGE...  8.64 us
    pallas_call x1, Pallas kernels, local(): pl.pallas_call(collect_kernel, out_shape=jax.ShapeDtypeStruct((members, b...  7.71 us
    all_to_all x1, starting transfers between devices, local(): lax.all_to_all(wanted.reshape(device_count, slot_count), ('face', 'tile')...  7.3 us
    all_to_all x1, waiting for transfers between devices, local(): lax.all_to_all(wanted.reshape(device_count, slot_count), ('face', 'tile')...  5.91 us
  transfers between devices with their start and end apart: 10, of which 2 were waited for; matrix products, arithmetic and copies ran while one was open for 1% of the time, Pallas kernels for 9%

profile of v2, /device:TPU:0, one launch (start us, length us, event | category | flops | bytes accessed | tf_op | source)
XLA Modules:
  0.0 133.5 jit_solution(12082013731928072081)
XLA Ops:
  0.0 0.0 copy-start.2
  0.0 0.0 copy-start.1
  0.0 0.0 copy-start
  0.0 0.7 broadcast_add_fusion.1
  0.7 0.1 copy.17
  0.8 0.1 sub.13
  1.0 0.8 copy.16
  1.7 0.1 reshape.77
  1.9 0.2 convert_reduce_fusion
  2.1 0.1 select_reduce_fusion
  2.2 0.7 add.52
  2.9 7.3 %all-to-all-start = ((s32[32,1,8]{2,1,0:T(1,128)}), s32[32,1,8]{2,1,0:T(1,128)S(1)}, u32[]{:S(2)}, u32[]{:S(2)}) async-start(s32[32,1,8]{2,1,0:T(1,128)} %bitcast), calls=%async_computation | async-start | bytes 32768 | tf_op jit(solution)/shard_map/all_to_all | solution.py:312
  10.2 1.1 copy.21
  11.3 5.9 %all-to-all-done = s32[32,1,8]{2,1,0:T(1,128)S(1)} async-done(((s32[32,1,8]{2,1,0:T(1,128)}), s32[32,1,8]{2,1,0:T(1,128)S(1)}, u32[]{:S(2)}, u32[]{:S(2)}) %all-to-all-start) | async-done | bytes 1056 | tf_op jit(solution)/shard_map/all_to_all | solution.py:312
  17.3 0.5 broadcast.71
  17.8 0.7 minimum_reduce_fusion
  18.5 0.1 min.26
  18.6 0.1 reshape.78.wanted
  18.7 0.8 gather_fusion
  19.6 1.7 %broadcast_select_fusion = bf16[256,16,128]{2,1,0:T(8,128)(2,1)} fusion(bf16[256,16,128]{2,1,0:T(8,128)(2,1)S(1)} %gather_fusion, pred[256]{0:T(512)(128)(4,1)S(1)} %compare_and_fusion), kind=kLoop, calls=%fused_computation.1 | loop fusion | flops 524288 | bytes 2097408 | tf_op jit(solution)/shard_map/jit(_take)/select_n | solution.py:317
  21.3 2.6 %all-to-all-start.1 = ((bf16[256,16,128]{2,1,0:T(8,128)(2,1)}), bf16[256,16,128]{2,1,0:T(8,128)(2,1)S(1)}, u32[]{:S(2)}, u32[]{:S(2)}) async-start(bf16[256,16,128]{2,1,0:T(8,128)(2,1)} %broadcast_select_fusion), calls=%async_computation.1 | async-start | bytes 2097152 | tf_op jit(solution)/shard_map/all_to_all | solution.py:318
  23.9 0.0 copy-done.2
  24.0 1.3 collective-permute-start.5
  25.3 4.5 %collective-permute-start.4 = (f32[8,256]{1,0:T(8,128)S(1)}, f32[8,256]{1,0:T(8,128)S(1)}, u32[]{:S(2)}, u32[]{:S(2)}) collective-permute-start(f32[8,256]{1,0:T(8,128)S(1)} %get-tuple-element.32), channel_id=1, source_target_pairs={{0,1},{1,2},{2,3},{3,4},{4,5},{5,6},{6,7},{8,9},{9,10},{10,11},{11... | collective-permute-start | bytes 24584 | tf_op jit(solution)/shard_map/ppermute | solution.py:285
  29.8 0.1 fusion.2
  29.9 0.1 reshape.80.tails
  30.0 0.1 reshape.79.heads
  30.1 0.9 collective-permute-start.7
  30.9 0.0 collective-permute-start.6
  30.9 20.6 %all-to-all-done.1.incoming = bf16[256,16,128]{2,1,0:T(8,128)(2,1)S(1)} async-done(((bf16[256,16,128]{2,1,0:T(8,128)(2,1)}), bf16[256,16,128]{2,1,0:T(8,128)(2,1)S(1)}, u32[]{:S(2)}, u32[]{:S(2)}) %all-to-all-start.1) | async-done | bytes 1048608 | tf_op jit(solution)/shard_map/all_to_all | solution.py:318
  51.5 0.0 copy-done.1
  51.5 0.0 copy-done
  51.5 4.0 %regrid.1 = (f32[64,16,128]{2,1,0:T(8,128)S(1)}, f32[2,16,128]{2,1,0:T(8,128)S(1)}, f32[2,16,128]{2,1,0:T(8,128)S(1)}) custom-call(s32[128]{0:T(128)S(1)} %multiply_add_fusion.place, bf16[256,16,128]{2,1,0:T(8,128)(2,1)S(1)} %all-to-all-done.1.incoming, s32[4,64,128]{2,1,0:T(8,128)S(1)} %copy-done, f32[4,64,128]{2,1,0:T(8,128)S(1)} %copy-done.1), custom_call_target="tpu_custom_call" | custom-call | tf_op jit(solution)/shard_map/regrid/pallas_call | solution.py:356
  55.5 1.3 collective-permute-start.1
  56.8 0.0 collective-permute-done.7.right
  56.8 4.6 %collective-permute-start = (f32[16,16,128]{2,1,0:T(8,128)S(1)}, f32[16,16,128]{2,1,0:T(8,128)S(1)}, u32[]{:S(2)}, u32[]{:S(2)}) collective-permute-start(f32[16,16,128]{2,1,0:T(8,128)S(1)} %get-tuple-element.28), channel_id=1, source_target_pairs={{0,1},{1,2},{2,3},{3,4},{4,5},{5,6},{6,7},{8,9},{9,10},{10,11},{11... | collective-permute-start | bytes 393224 | tf_op jit(solution)/shard_map/ppermute | solution.py:285
  61.4 0.1 pad_add_fusion.edge
  61.5 0.0 collective-permute-done.6.left
  61.5 0.0 collective-permute-start.3
  61.5 0.0 collective-permute-done.5.below
  61.5 0.5 collective-permute-start.2
  62.0 0.0 collective-permute-done.4.above
  62.0 8.6 %prepare.1 = (f32[16,40,128]{2,1,0:T(8,128)S(1)}, f32[16,32,128]{2,1,0:T(8,128)S(1)}, f32[8,2,128]{2,1,0:T(2,128)S(1)}, f32[8,2,128]{2,1,0:T(2,128)S(1)}, bf16[6...) custom-call(f32[32,256]{1,0:T(8,128)S(1)} %copy-done.2, f32[8,256]{1,0:T(8,128)S(1)} %collective-permute-done.4.above, ...), custom_call_target="tpu_custom_call" | custom-call | flops 1000000000 | bytes 16777216 | tf_op jit(solution)/shard_map/prepare/pallas_call | solution.py:331
  70.6 0.0 collective-permute-done.3.right_heads
  70.7 0.0 collective-permute-done.2.left_tails
  70.7 0.0 collective-permute-done.1.below
  70.7 0.0 collective-permute-done.above
  70.7 22.1 %score.1 = s16[32,9,16,128]{3,2,1,0:T(8,128)(2,1)S(1)} custom-call(s32[2]{0:T(128)S(1)} %pad_add_fusion.edge, s32[128]{0:T(128)S(1)} %multiply_add_fusion.place, f32[64,16,128]{2,1,0:T(8,128)S(1)} %get-tuple-element.15.field, f32[16,16,128]{2,1,0:T(8,128)S(1)} %collective-permute-done.above, f32[16,16,128]{2,1,0:T(8,128)S(1)} %collective-permute-done.1.below, ...), custom_call_target="tpu_custom_call" | custom-call | tf_op jit(solution)/shard_map/score/pallas_call | solution.py:376
  92.8 33.0 %all_to_all.16.returned = s16[32,9,16,128]{3,2,1,0:T(8,128)(2,1)S(1)} all-to-all(s16[32,9,16,128]{3,2,1,0:T(8,128)(2,1)S(1)} %score.1), channel_id=1, replica_groups=mesh['face'=4,'tile'=8] {'face','tile'}, dimensions={0} | all-to-all | bytes 2359296 | tf_op jit(solution)/shard_map/all_to_all | solution.py:395
  125.8 7.7 %collect.1 = f32[16,64,128]{2,1,0:T(8,128)} custom-call(s32[256]{0:T(256)S(1)} %reshape.78.wanted, s16[32,9,16,128]{3,2,1,0:T(8,128)(2,1)S(1)} %all_to_all.16.returned), custom_call_target="tpu_custom_call" | custom-call | tf_op jit(solution)/shard_map/collect/pallas_call | solution.py:398
  (7 shorter events, 0.1 us)
Async XLA Ops:
  0.0 23.9 %copy-start.2 = (f32[32,256]{1,0:T(8,128)S(1)}, f32[32,256]{1,0:T(8,128)}, u32[]{:S(2)}) copy-start(f32[32,256]{1,0:T(8,128)} %truth) | copy-start | bytes 98308
  0.0 51.5 %copy-start.1 = (f32[4,64,128]{2,1,0:T(8,128)S(1)}, f32[4,64,128]{2,1,0:T(8,128)}, u32[]{:S(2)}) copy-start(f32[4,64,128]{2,1,0:T(8,128)} %factors.3) | copy-start | bytes 393220
  0.0 51.5 %copy-start = (s32[4,64,128]{2,1,0:T(8,128)S(1)}, s32[4,64,128]{2,1,0:T(8,128)}, u32[]{:S(2)}) copy-start(s32[4,64,128]{2,1,0:T(8,128)} %positions.3) | copy-start | bytes 393220
  2.9 14.3 %all-to-all-start = ((s32[32,1,8]{2,1,0:T(1,128)}), s32[32,1,8]{2,1,0:T(1,128)S(1)}, u32[]{:S(2)}, u32[]{:S(2)}) async-start(s32[32,1,8]{2,1,0:T(1,128)} %bitcast), calls=%async_computation | async-start | bytes 32768 | tf_op jit(solution)/shard_map/all_to_all | solution.py:312
  21.3 30.2 %all-to-all-start.1 = ((bf16[256,16,128]{2,1,0:T(8,128)(2,1)}), bf16[256,16,128]{2,1,0:T(8,128)(2,1)S(1)}, u32[]{:S(2)}, u32[]{:S(2)}) async-start(bf16[256,16,128]{2,1,0:T(8,128)(2,1)} %broadcast_select_fusion), calls=%async_computation.1 | async-start | bytes 2097152 | tf_op jit(solution)/shard_map/all_to_all | solution.py:318
  24.0 37.5 %collective-permute-start.5 = (f32[8,256]{1,0:T(8,128)S(1)}, f32[8,256]{1,0:T(8,128)S(1)}, u32[]{:S(2)}, u32[]{:S(2)}) collective-permute-start(f32[8,256]{1,0:T(8,128)S(1)} %get-tuple-element.31), channel_id=1, source_target_pairs={{1,0},{2,1},{3,2},{4,3},{5,4},{6,5},{7,6},{9,8},{10,9},{11,10},{12... | collective-permute-start | bytes 24584 | tf_op jit(solution)/shard_map/ppermute | solution.py:285
  25.3 36.7 %collective-permute-start.4 = (f32[8,256]{1,0:T(8,128)S(1)}, f32[8,256]{1,0:T(8,128)S(1)}, u32[]{:S(2)}, u32[]{:S(2)}) collective-permute-start(f32[8,256]{1,0:T(8,128)S(1)} %get-tuple-element.32), channel_id=1, source_target_pairs={{0,1},{1,2},{2,3},{3,4},{4,5},{5,6},{6,7},{8,9},{9,10},{10,11},{11... | collective-permute-start | bytes 24584 | tf_op jit(solution)/shard_map/ppermute | solution.py:285
  30.1 26.8 %collective-permute-start.7 = (f32[2,128]{1,0:T(2,128)S(1)}, f32[2,128]{1,0:T(2,128)S(1)}, u32[]{:S(2)}, u32[]{:S(2)}) collective-permute-start(f32[2,128]{1,0:T(2,128)S(1)} %reshape.79.heads), channel_id=1, source_target_pairs={{8,0},{16,8},{24,16},{0,24},{9,1},{17,9},{25,17},{1,25},{10,2},{18... | collective-permute-start | bytes 3080 | tf_op jit(solution)/shard_map/ppermute | solution.py:285
  30.9 30.5 %collective-permute-start.6 = (f32[2,128]{1,0:T(2,128)S(1)}, f32[2,128]{1,0:T(2,128)S(1)}, u32[]{:S(2)}, u32[]{:S(2)}) collective-permute-start(f32[2,128]{1,0:T(2,128)S(1)} %reshape.80.tails), channel_id=1, source_target_pairs={{0,8},{8,16},{16,24},{24,0},{1,9},{9,17},{17,25},{25,1},{2,10},{10... | collective-permute-start | bytes 3080 | tf_op jit(solution)/shard_map/ppermute | solution.py:285
  55.5 15.1 %collective-permute-start.1 = (f32[16,16,128]{2,1,0:T(8,128)S(1)}, f32[16,16,128]{2,1,0:T(8,128)S(1)}, u32[]{:S(2)}, u32[]{:S(2)}) collective-permute-start(f32[16,16,128]{2,1,0:T(8,128)S(1)} %get-tuple-element.27), channel_id=1, source_target_pairs={{1,0},{2,1},{3,2},{4,3},{5,4},{6,5},{7,6},{9,8},{10,9},{11,10},{12... | collective-permute-start | bytes 393224 | tf_op jit(solution)/shard_map/ppermute | solution.py:285
  56.8 13.8 %collective-permute-start = (f32[16,16,128]{2,1,0:T(8,128)S(1)}, f32[16,16,128]{2,1,0:T(8,128)S(1)}, u32[]{:S(2)}, u32[]{:S(2)}) collective-permute-start(f32[16,16,128]{2,1,0:T(8,128)S(1)} %get-tuple-element.28), channel_id=1, source_target_pairs={{0,1},{1,2},{2,3},{3,4},{4,5},{5,6},{6,7},{8,9},{9,10},{10,11},{11... | collective-permute-start | bytes 393224 | tf_op jit(solution)/shard_map/ppermute | solution.py:285
  61.5 9.2 %collective-permute-start.3 = (f32[2,16,128]{2,1,0:T(8,128)S(1)}, f32[2,16,128]{2,1,0:T(8,128)S(1)}, u32[]{:S(2)}, u32[]{:S(2)}) collective-permute-start(f32[2,16,128]{2,1,0:T(8,128)S(1)} %get-tuple-element.16.heads), channel_id=1, source_target_pairs={{8,0},{16,8},{24,16},{0,24},{9,1},{17,9},{25,17},{1,25},{10,2},{18... | collective-permute-start | bytes 49160 | tf_op jit(solution)/shard_map/ppermute | solution.py:285
  61.5 9.2 %collective-permute-start.2 = (f32[2,16,128]{2,1,0:T(8,128)S(1)}, f32[2,16,128]{2,1,0:T(8,128)S(1)}, u32[]{:S(2)}, u32[]{:S(2)}) collective-permute-start(f32[2,16,128]{2,1,0:T(8,128)S(1)} %get-tuple-element.17.tails), channel_id=1, source_target_pairs={{0,8},{8,16},{16,24},{24,0},{1,9},{9,17},{17,25},{25,1},{2,10},{10... | collective-permute-start | bytes 49160 | tf_op jit(solution)/shard_map/ppermute | solution.py:285

commit v3 on v2

--- a/solution.py
+++ b/solution.py
@@ -30,6 +30,77 @@
 
 def lane_ids():
     return lax.broadcasted_iota(jnp.int32, (16, LANES), 1)
+
+
+def place_of(number, tiles):
+    return (number // tiles, number % tiles)
+
+
+def greet(count, tiles, me):
+    barrier = pltpu.get_barrier_semaphore()
+
+    def step(s, carry):
+        other = (me + s) % count
+        pl.semaphore_signal(
+            barrier, inc=1, device_id=place_of(other, tiles), device_id_type=pl.DeviceIdType.MESH
+        )
+        return carry
+
+    lax.fori_loop(1, count, step, 0)
+    pl.semaphore_wait(barrier, count - 1)
+
+
+def remote(source, target, sent, arrived, other, tiles):
+    return pltpu.make_async_remote_copy(
+        src_ref=source, dst_ref=target, send_sem=sent, recv_sem=arrived,
+        device_id=place_of(other, tiles), device_id_type=pl.DeviceIdType.MESH,
+    )
+
+
+def fetch_kernel(
+    count, tiles, wanted, strips, incoming, asked,
+    asked_rows, numbers, outgoing, list_sent, list_got, strip_sent, strip_got, local_sem,
+):
+    me = lax.axis_index("face") * tiles + lax.axis_index("tile")
+    slot_count = outgoing.shape[1]
+    bands = strips.shape[0]
+    greet(count, tiles, me)
+
+    def ask(s, carry):
+        other = (me + s) % count
+        remote(wanted.at[other], asked_rows.at[me], list_sent.at[s], list_got.at[s], other, tiles).start()
+        return carry
+
+    def heard(s, carry):
+        other = (me + s) % count
+        remote(wanted.at[other], asked_rows.at[me], list_sent.at[s], list_got.at[s], other, tiles).wait()
+        return carry
+
+    lax.fori_loop(1, count, ask, 0)
+    asked_rows[me] = wanted[me]
+    lax.fori_loop(1, count, heard, 0)
+    listing = pltpu.make_async_copy(asked_rows, numbers, local_sem)
+    listing.start()
+    asked[...] = asked_rows[...]
+    listing.wait()
+
+    for k in range(slot_count):
+        incoming[me, k] = strips[jnp.minimum(numbers[me, 0, k], bands - 1)]
+
+    def send(s, carry):
+        other = (me + s) % count
+        for k in range(slot_count):
+            outgoing[s, k] = strips[jnp.minimum(numbers[other, 0, k], bands - 1)]
+        remote(outgoing.at[s], incoming.at[me], strip_sent.at[s], strip_got.at[s], other, tiles).start()
+        return carry
+
+    def got(s, carry):
+        other = (me + s) % count
+        remote(outgoing.at[s], incoming.at[me], strip_sent.at[s], strip_got.at[s], other, tiles).wait()
+        return carry
+
+    lax.fori_loop(1, count, send, 0)
+    lax.fori_loop(1, count, got, 0)
 
 
 def regrid_kernel(place, incoming, positions, factors, field, heads, tails, weights):
@@ -267,7 +338,7 @@
             summed[at] = summed[at] + code * step_of[:, k : k + 1]
         return carry
 
-    lax.fori_loop(0, returned.shape[0], step, 0)
+    lax.fori_loop(0, returned.shape[0], step, 0, unroll=4)
     for g in range(bands):
         slope[:, g, :] = summed[g]
 
@@ -309,15 +380,35 @@
     wanted = bands + jnp.sum(
         jnp.where(held, parent_band_slot.reshape(-1)[None, :] - bands, 0), axis=1
     )
-    asked = lax.all_to_all(
-        wanted.reshape(device_count, slot_count), ("face", "tile"),
-        split_axis=0, concat_axis=0, tiled=True,
-    ).reshape(-1)
     strips = jnp.transpose(predicted_field, (1, 0, 2))
-    outgoing = jnp.take(strips, jnp.minimum(asked, bands - 1), axis=0)
-    incoming = lax.all_to_all(
-        outgoing, ("face", "tile"), split_axis=0, concat_axis=0, tiled=True
-    )
+    lists = jnp.pad(
+        wanted.reshape(device_count, 1, slot_count), ((0, 0), (0, 0), (0, LANES - slot_count))
+    )
+    incoming, asked = pl.pallas_call(
+        functools.partial(fetch_kernel, device_count, tile_count),
+        out_shape=(
+            jax.ShapeDtypeStruct((device_count, slot_count, members, pixels), predicted_field.dtype),
+            jax.ShapeDtypeStruct((device_count, 1, LANES), jnp.int32),
+        ),
+        in_specs=[spec(VMEM), spec(VMEM)],
+        out_specs=(spec(VMEM), spec(VMEM)),
+        scratch_shapes=[
+            pltpu.VMEM((device_count, 1, LANES), jnp.int32),
+            pltpu.SMEM((device_count, 1, LANES), jnp.int32),
+            pltpu.VMEM((device_count, slot_count, members, pixels), predicted_field.dtype),
+            pltpu.SemaphoreType.DMA((device_count,)),
+            pltpu.SemaphoreType.DMA((device_count,)),
+            pltpu.SemaphoreType.DMA((device_count,)),
+            pltpu.SemaphoreType.DMA((device_count,)),
+            pltpu.SemaphoreType.DMA,
+        ],
+        compiler_params=pltpu.CompilerParams(
+            collective_id=1, has_side_effects=True, vmem_limit_bytes=24 << 20
+        ),
+        name="fetch",
+    )(lists, strips)
+    incoming = incoming.reshape(slots_all, members, pixels)
+    asked = asked[:, 0, :slot_count].reshape(-1)
 
     truth_field, asked_late = lax.optimization_barrier((truth_field, asked))
     truth_above = shifted(truth_field[rows - RANGE :], "tile", 1, False)

time: 134 us -> 136 us (1.015)
  Pallas kernels: 42.4 us -> 76.9 us
  waiting for transfers between devices: 26.5 us -> 0.02 us
  starting transfers between devices: 23 us -> 13.4 us
  local copies, waits for them, and re-layouts: 4.78 us -> 8.6 us
  other arithmetic: 3.57 us -> 1.06 us
  blocking collectives: 33 us -> 35.1 us
    pallas_call x0 -> x1, Pallas kernels: none -> 37 us  [local(): pl.pallas_call(functools.partial(fetch_kernel, device_count, tile_count),...]
    all_to_all x2 -> x0, waiting for transfers between devices: 26.5 us -> none  [the longest x1 20.6 us: local(): lax.all_to_all(outgoing, ('face', 'tile'), split_axis=0, concat_axis=0, t...]
    all_to_all x2 -> x0, starting transfers between devices: 9.94 us -> none  [the longest x1 7.3 us: local(): lax.all_to_all(wanted.reshape(device_count, slot_count), ('face', 'tile')...]
    unnamed x8 -> x12, local copies, waits for them, and re-layouts: 1.91 us -> 6.28 us
    pallas_call x1, Pallas kernels: 7.71 us -> 5.16 us  [local(): pl.pallas_call(collect_kernel, out_shape=jax.ShapeDtypeStruct((members, b...]
    all_to_all x1, blocking collectives: 33 us -> 35.1 us  [local(): lax.all_to_all(slots, ('face', 'tile'), split_axis=0, concat_axis=0, tile...]
    select_n x2 -> x0, other arithmetic: 1.71 us -> none  [local(): outgoing = jnp.take(strips, jnp.minimum(asked, bands - 1), axis=0)]
  transfers between devices with their start and end apart: 10 -> 8, of which waited for: 2 -> 0; matrix products, arithmetic and copies ran while one was open for 1% -> 1% of each run, Pallas kernels for 9% -> 9%
where the time goes in v3:
time: 136 us; the launch traced here: 135 us
  Pallas kernels  76.9 us (57%)
  blocking collectives  35.1 us (26%)
  starting transfers between devices  13.4 us (10%)
  local copies, waits for them, and re-layouts  8.6 us (6%)
    pallas_call x1, Pallas kernels, local(): pl.pallas_call(functools.partial(fetch_kernel, device_count, tile_count),...  37 us
    all_to_all x1, blocking collectives, local(): lax.all_to_all(slots, ('face', 'tile'), split_axis=0, concat_axis=0, tile...  35.1 us
    pallas_call x1, Pallas kernels, local(): pl.pallas_call(score_kernel, out_shape=jax.ShapeDtypeStruct((device_count...  22.1 us
    ppermute x8, starting transfers between devices, shifted(): return lax.ppermute(cells, axis, pairs)  13.4 us
    pallas_call x1, Pallas kernels, local(): pl.pallas_call(prepare_kernel, out_shape=(jax.ShapeDtypeStruct((2 * RANGE...  8.64 us
    unnamed x12, local copies, waits for them, and re-layouts  6.28 us
    pallas_call x1, Pallas kernels, local(): pl.pallas_call(collect_kernel, out_shape=jax.ShapeDtypeStruct((members, b...  5.16 us
    pallas_call x1, Pallas kernels, local(): pl.pallas_call(regrid_kernel, out_shape=(jax.ShapeDtypeStruct((bands, mem...  3.97 us
  transfers between devices with their start and end apart: 8, of which 0 were waited for; matrix products, arithmetic and copies ran while one was open for 1% of the time, Pallas kernels for 9%

profile of v3, /device:TPU:0, one launch (start us, length us, event | category | flops | bytes accessed | tf_op | source)
XLA Modules:
  0.0 135.2 jit_solution(3672154002043473340)
XLA Ops:
  0.0 0.7 broadcast_add_fusion.1
  0.7 0.1 copy.15
  0.8 0.1 sub.13
  0.9 0.8 copy.14
  1.7 0.1 reshape.44
  1.8 0.2 convert_reduce_fusion
  2.0 0.1 select_reduce_fusion
  2.2 0.1 add.34
  2.2 1.1 copy.19
  3.4 37.0 %fetch.1 = (bf16[32,8,16,128]{3,2,1,0:T(8,128)(2,1)S(1)}, s32[32,1,128]{2,1,0:T(1,128)S(1)}) custom-call(s32[32,1,128]{2,1,0:T(1,128)S(1)} %pad.4.wanted, bf16[64,16,128]{2,1,0:T(8,128)(2,1)S(1)} %bitcast.8), custom_call_target="tpu_custom_call" | custom-call | tf_op jit(solution)/shard_map/fetch/pallas_call | solution.py:387
  40.4 0.1 reshape_squeeze.3.wanted
  40.5 0.7 fusion.3
  41.2 1.3 collective-permute-start.5
  42.5 4.5 %collective-permute-start.4 = (f32[8,256]{1,0:T(8,128)S(1)}, f32[8,256]{1,0:T(8,128)S(1)}, u32[]{:S(2)}, u32[]{:S(2)}) collective-permute-start(f32[8,256]{1,0:T(8,128)S(1)} %get-tuple-element.34), channel_id=1, source_target_pairs={{0,1},{1,2},{2,3},{3,4},{4,5},{5,6},{6,7},{8,9},{9,10},{10,11},{11... | collective-permute-start | bytes 24584 | tf_op jit(solution)/shard_map/ppermute | solution.py:356
  47.1 0.8 fusion.2
  47.9 0.1 reshape.46.heads
  48.0 0.1 collective-permute-start.7
  48.0 0.1 reshape.47.tails
  48.1 0.5 collective-permute-start.6
  48.7 0.0 copy-start
  48.7 0.9 copy-done
  49.6 0.0 copy-start.2
  49.6 0.9 copy-done.2
  50.5 4.0 %regrid.1 = (f32[64,16,128]{2,1,0:T(8,128)S(1)}, f32[2,16,128]{2,1,0:T(8,128)S(1)}, f32[2,16,128]{2,1,0:T(8,128)S(1)}) custom-call(s32[128]{0:T(128)S(1)} %multiply_add_fusion.place, bf16[256,16,128]{2,1,0:T(8,128)(2,1)S(1)} %bitcast.7, s32[4,64,128]{2,1,0:T(8,128)S(1)} %copy-done, f32[4,64,128]{2,1,0:T(8,128)S(1)} %copy-done.2), custom_call_target="tpu_custom_call" | custom-call | tf_op jit(solution)/shard_map/regrid/pallas_call | solution.py:447
  54.5 1.3 collective-permute-start.1
  55.8 0.0 collective-permute-done.7.right
  55.8 4.7 %collective-permute-start = (f32[16,16,128]{2,1,0:T(8,128)S(1)}, f32[16,16,128]{2,1,0:T(8,128)S(1)}, u32[]{:S(2)}, u32[]{:S(2)}) collective-permute-start(f32[16,16,128]{2,1,0:T(8,128)S(1)} %get-tuple-element.30), channel_id=1, source_target_pairs={{0,1},{1,2},{2,3},{3,4},{4,5},{5,6},{6,7},{8,9},{9,10},{10,11},{11... | collective-permute-start | bytes 393224 | tf_op jit(solution)/shard_map/ppermute | solution.py:356
  60.5 0.1 pad_add_fusion.edge
  60.6 0.0 collective-permute-done.6.left
  60.6 1.0 collective-permute-start.3
  61.5 0.0 collective-permute-done.5.below
  61.5 0.0 collective-permute-start.2
  61.5 0.0 collective-permute-done.4.above
  61.5 0.0 copy-start.1
  61.6 0.9 copy-done.1
  62.5 0.0 copy-start.3
  62.5 0.9 copy-done.3
  63.4 0.0 copy-start.4
  63.4 0.8 copy-done.4
  64.1 8.6 %prepare.1 = (f32[16,40,128]{2,1,0:T(8,128)S(1)}, f32[16,32,128]{2,1,0:T(8,128)S(1)}, f32[8,2,128]{2,1,0:T(2,128)S(1)}, f32[8,2,128]{2,1,0:T(2,128)S(1)}, bf16[6...) custom-call(f32[32,256]{1,0:T(8,128)S(1)} %copy-done.4, f32[8,256]{1,0:T(8,128)S(1)} %collective-permute-done.4.above, ...), custom_call_target="tpu_custom_call" | custom-call | flops 1000000000 | bytes 16777216 | tf_op jit(solution)/shard_map/prepare/pallas_call | solution.py:422
  72.8 0.0 collective-permute-done.3.right_heads
  72.8 0.0 collective-permute-done.2.left_tails
  72.8 0.0 collective-permute-done.1.below
  72.8 0.0 collective-permute-done.above
  72.8 22.1 %score.1 = s16[32,9,16,128]{3,2,1,0:T(8,128)(2,1)S(1)} custom-call(s32[2]{0:T(128)S(1)} %pad_add_fusion.edge, s32[128]{0:T(128)S(1)} %multiply_add_fusion.place, f32[64,16,128]{2,1,0:T(8,128)S(1)} %get-tuple-element.19.field, f32[16,16,128]{2,1,0:T(8,128)S(1)} %collective-permute-done.above, f32[16,16,128]{2,1,0:T(8,128)S(1)} %collective-permute-done.1.below, ...), custom_call_target="tpu_custom_call" | custom-call | tf_op jit(solution)/shard_map/score/pallas_call | solution.py:467
  94.9 35.1 %all_to_all.5.returned = s16[32,9,16,128]{3,2,1,0:T(8,128)(2,1)S(1)} all-to-all(s16[32,9,16,128]{3,2,1,0:T(8,128)(2,1)S(1)} %score.1), channel_id=1, replica_groups=mesh['face'=4,'tile'=8] {'face','tile'}, dimensions={0} | all-to-all | bytes 2359296 | tf_op jit(solution)/shard_map/all_to_all | solution.py:486
  130.0 5.2 %collect.1 = f32[16,64,128]{2,1,0:T(8,128)} custom-call(s32[256]{0:T(256)S(1)} %reshape_squeeze.3.wanted, s16[32,9,16,128]{3,2,1,0:T(8,128)(2,1)S(1)} %all_to_all.5.returned), custom_call_target="tpu_custom_call" | custom-call | tf_op jit(solution)/shard_map/collect/pallas_call | solution.py:489
  (5 shorter events, 0.1 us)
Async XLA Ops:
  41.2 20.3 %collective-permute-start.5 = (f32[8,256]{1,0:T(8,128)S(1)}, f32[8,256]{1,0:T(8,128)S(1)}, u32[]{:S(2)}, u32[]{:S(2)}) collective-permute-start(f32[8,256]{1,0:T(8,128)S(1)} %get-tuple-element.33), channel_id=1, source_target_pairs={{1,0},{2,1},{3,2},{4,3},{5,4},{6,5},{7,6},{9,8},{10,9},{11,10},{12... | collective-permute-start | bytes 24584 | tf_op jit(solution)/shard_map/ppermute | solution.py:356
  42.5 19.0 %collective-permute-start.4 = (f32[8,256]{1,0:T(8,128)S(1)}, f32[8,256]{1,0:T(8,128)S(1)}, u32[]{:S(2)}, u32[]{:S(2)}) collective-permute-start(f32[8,256]{1,0:T(8,128)S(1)} %get-tuple-element.34), channel_id=1, source_target_pairs={{0,1},{1,2},{2,3},{3,4},{4,5},{5,6},{6,7},{8,9},{9,10},{10,11},{11... | collective-permute-start | bytes 24584 | tf_op jit(solution)/shard_map/ppermute | solution.py:356
  48.0 7.8 %collective-permute-start.7 = (f32[2,128]{1,0:T(2,128)S(1)}, f32[2,128]{1,0:T(2,128)S(1)}, u32[]{:S(2)}, u32[]{:S(2)}) collective-permute-start(f32[2,128]{1,0:T(2,128)S(1)} %reshape.46.heads), channel_id=1, source_target_pairs={{8,0},{16,8},{24,16},{0,24},{9,1},{17,9},{25,17},{1,25},{10,2},{18... | collective-permute-start | bytes 3080 | tf_op jit(solution)/shard_map/ppermute | solution.py:356
  48.1 12.4 %collective-permute-start.6 = (f32[2,128]{1,0:T(2,128)S(1)}, f32[2,128]{1,0:T(2,128)S(1)}, u32[]{:S(2)}, u32[]{:S(2)}) collective-permute-start(f32[2,128]{1,0:T(2,128)S(1)} %reshape.47.tails), channel_id=1, source_target_pairs={{0,8},{8,16},{16,24},{24,0},{1,9},{9,17},{17,25},{25,1},{2,10},{10... | collective-permute-start | bytes 3080 | tf_op jit(solution)/shard_map/ppermute | solution.py:356
  48.7 0.9 copy-start
  49.6 0.9 copy-start.2
  54.5 18.3 %collective-permute-start.1 = (f32[16,16,128]{2,1,0:T(8,128)S(1)}, f32[16,16,128]{2,1,0:T(8,128)S(1)}, u32[]{:S(2)}, u32[]{:S(2)}) collective-permute-start(f32[16,16,128]{2,1,0:T(8,128)S(1)} %get-tuple-element.29), channel_id=1, source_target_pairs={{1,0},{2,1},{3,2},{4,3},{5,4},{6,5},{7,6},{9,8},{10,9},{11,10},{12... | collective-permute-start | bytes 393224 | tf_op jit(solution)/shard_map/ppermute | solution.py:356
  55.8 17.0 %collective-permute-start = (f32[16,16,128]{2,1,0:T(8,128)S(1)}, f32[16,16,128]{2,1,0:T(8,128)S(1)}, u32[]{:S(2)}, u32[]{:S(2)}) collective-permute-start(f32[16,16,128]{2,1,0:T(8,128)S(1)} %get-tuple-element.30), channel_id=1, source_target_pairs={{0,1},{1,2},{2,3},{3,4},{4,5},{5,6},{6,7},{8,9},{9,10},{10,11},{11... | collective-permute-start | bytes 393224 | tf_op jit(solution)/shard_map/ppermute | solution.py:356
  60.6 12.2 %collective-permute-start.3 = (f32[2,16,128]{2,1,0:T(8,128)S(1)}, f32[2,16,128]{2,1,0:T(8,128)S(1)}, u32[]{:S(2)}, u32[]{:S(2)}) collective-permute-start(f32[2,16,128]{2,1,0:T(8,128)S(1)} %get-tuple-element.20.heads), channel_id=1, source_target_pairs={{8,0},{16,8},{24,16},{0,24},{9,1},{17,9},{25,17},{1,25},{10,2},{18... | collective-permute-start | bytes 49160 | tf_op jit(solution)/shard_map/ppermute | solution.py:356
  61.5 11.2 %collective-permute-start.2 = (f32[2,16,128]{2,1,0:T(8,128)S(1)}, f32[2,16,128]{2,1,0:T(8,128)S(1)}, u32[]{:S(2)}, u32[]{:S(2)}) collective-permute-start(f32[2,16,128]{2,1,0:T(8,128)S(1)} %get-tuple-element.21.tails), channel_id=1, source_target_pairs={{0,8},{8,16},{16,24},{24,0},{1,9},{9,17},{17,25},{25,1},{2,10},{10... | collective-permute-start | bytes 49160 | tf_op jit(solution)/shard_map/ppermute | solution.py:356
  61.5 0.9 copy-start.1
  62.5 0.9 copy-start.3
  63.4 0.8 copy-start.4

commit v4 on v3

--- a/solution.py
+++ b/solution.py
@@ -58,8 +58,10 @@
 
 
 def fetch_kernel(
-    count, tiles, wanted, strips, incoming, asked,
+    count, tiles, wanted, strips, truth, heads, tails, positions, factors,
+    incoming, asked, root_tall, root_wide, root_left, root_right, high_far, low_far,
     asked_rows, numbers, outgoing, list_sent, list_got, strip_sent, strip_got, local_sem,
+    tall, left, right, high, low, weights, edge_sent, edge_got, stored,
 ):
     me = lax.axis_index("face") * tiles + lax.axis_index("tile")
     slot_count = outgoing.shape[1]
@@ -78,6 +80,24 @@
 
     lax.fori_loop(1, count, ask, 0)
     asked_rows[me] = wanted[me]
+    rows = truth.shape[0]
+    faces = count // tiles
+    face, tile = lax.axis_index("face"), lax.axis_index("tile")
+    north = face * tiles + (tile + 1) % tiles
+    south = face * tiles + (tile + tiles - 1) % tiles
+    east = ((face + 1) % faces) * tiles + tile
+    west = ((face + faces - 1) % faces) * tiles + tile
+    edges = []
+    for i, (source, target, other) in enumerate((
+        (truth.at[pl.ds(rows - RANGE, RANGE)], tall.at[pl.ds(0, RANGE)], north),
+        (truth.at[pl.ds(0, RANGE)], tall.at[pl.ds(rows + RANGE, RANGE)], south),
+        (tails, left, east),
+        (heads, right, west),
+    )):
+        edges.append(remote(source, target, edge_sent.at[i], edge_got.at[i], other, tiles))
+    for edge in edges:
+        edge.start()
+    tall[pl.ds(RANGE, rows)] = truth[...]
     lax.fori_loop(1, count, heard, 0)
     listing = pltpu.make_async_copy(asked_rows, numbers, local_sem)
     listing.start()
@@ -100,7 +120,19 @@
         return carry
 
     lax.fori_loop(1, count, send, 0)
+    for edge in edges:
+        edge.wait()
+    prepare(
+        truth, heads, tails, left, right, positions, factors,
+        root_tall, root_wide, root_left, root_right, high, low, tall, weights,
+    )
+    store_high = pltpu.make_async_copy(high, high_far, stored.at[0])
+    store_low = pltpu.make_async_copy(low, low_far, stored.at[1])
+    store_high.start()
+    store_low.start()
     lax.fori_loop(1, count, got, 0)
+    store_high.wait()
+    store_low.wait()
 
 
 def regrid_kernel(place, incoming, positions, factors, field, heads, tails, weights):
@@ -149,14 +181,11 @@
     return mismatch * (diff * (root * inverse * inverse))
 
 
-def prepare_kernel(
-    truth, above, below, heads, tails, left, right, positions, factors,
+def prepare(
+    truth, heads, tails, left, right, positions, factors,
     root_tall, root_wide, root_left, root_right, high, low, tall, weights,
 ):
     rows = truth.shape[0]
-    tall[pl.ds(0, RANGE)] = above[...]
-    tall[pl.ds(RANGE, rows)] = truth[...]
-    tall[pl.ds(RANGE + rows, RANGE)] = below[...]
     span = rows + RANGE
     for k in range(1, RANGE + 1):
         root = root_of(tall[pl.ds(0, span), :] - tall[pl.ds(k, span), :])
@@ -384,14 +413,24 @@
     lists = jnp.pad(
         wanted.reshape(device_count, 1, slot_count), ((0, 0), (0, 0), (0, LANES - slot_count))
     )
-    incoming, asked = pl.pallas_call(
+    truth_heads = truth_field[:, :RANGE].reshape(groups, LANES)
+    truth_tails = truth_field[:, cols - RANGE :].reshape(groups, LANES)
+    f32 = jnp.float32
+    matrices = jax.ShapeDtypeStruct((bands, pixels, 2 * pixels), jnp.bfloat16)
+    incoming, asked, root_tall, root_wide, root_left, root_right, high, low = pl.pallas_call(
         functools.partial(fetch_kernel, device_count, tile_count),
         out_shape=(
             jax.ShapeDtypeStruct((device_count, slot_count, members, pixels), predicted_field.dtype),
             jax.ShapeDtypeStruct((device_count, 1, LANES), jnp.int32),
+            jax.ShapeDtypeStruct((2 * RANGE, rows + RANGE, LANES), f32),
+            jax.ShapeDtypeStruct((2 * RANGE, rows, LANES), f32),
+            jax.ShapeDtypeStruct((RANGE, groups, LANES), f32),
+            jax.ShapeDtypeStruct((RANGE, groups, LANES), f32),
+            matrices,
+            matrices,
         ),
-        in_specs=[spec(VMEM), spec(VMEM)],
-        out_specs=(spec(VMEM), spec(VMEM)),
+        in_specs=[spec(VMEM)] * 7,
+        out_specs=(spec(VMEM),) * 6 + (spec(pl.ANY),) * 2,
         scratch_shapes=[
             pltpu.VMEM((device_count, 1, LANES), jnp.int32),
             pltpu.SMEM((device_count, 1, LANES), jnp.int32),
@@ -401,47 +440,26 @@
             pltpu.SemaphoreType.DMA((device_count,)),
             pltpu.SemaphoreType.DMA((device_count,)),
             pltpu.SemaphoreType.DMA,
+            pltpu.VMEM((rows + 2 * RANGE, cols), f32),
+            pltpu.VMEM((groups, LANES), f32),
+            pltpu.VMEM((groups, LANES), f32),
+            pltpu.VMEM(matrices.shape, matrices.dtype),
+            pltpu.VMEM(matrices.shape, matrices.dtype),
+            pltpu.VMEM((4, bands, pixels), f32),
+            pltpu.SemaphoreType.DMA((4,)),
+            pltpu.SemaphoreType.DMA((4,)),
+            pltpu.SemaphoreType.DMA((2,)),
         ],
         compiler_params=pltpu.CompilerParams(
-            collective_id=1, has_side_effects=True, vmem_limit_bytes=24 << 20
+            collective_id=1, has_side_effects=True, vmem_limit_bytes=40 << 20
         ),
         name="fetch",
-    )(lists, strips)
+    )(
+        lists, strips, truth_field, truth_heads, truth_tails,
+        neighbour_positions, unscaled_neighbour_factor,
+    )
     incoming = incoming.reshape(slots_all, members, pixels)
     asked = asked[:, 0, :slot_count].reshape(-1)
-
-    truth_field, asked_late = lax.optimization_barrier((truth_field, asked))
-    truth_above = shifted(truth_field[rows - RANGE :], "tile", 1, False)
-    truth_below = shifted(truth_field[:RANGE], "tile", -1, False)
-    truth_heads = truth_field[:, :RANGE].reshape(groups, LANES)
-    truth_tails = truth_field[:, cols - RANGE :].reshape(groups, LANES)
-    truth_left = shifted(truth_tails, "face", 1, True)
-    truth_right = shifted(truth_heads, "face", -1, True)
-    f32 = jnp.float32
-    matrices = jax.ShapeDtypeStruct((bands, pixels, 2 * pixels), jnp.bfloat16)
-    root_tall, root_wide, root_left, root_right, high, low = pl.pallas_call(
-        prepare_kernel,
-        out_shape=(
-            jax.ShapeDtypeStruct((2 * RANGE, rows + RANGE, LANES), f32),
-            jax.ShapeDtypeStruct((2 * RANGE, rows, LANES), f32),
-            jax.ShapeDtypeStruct((RANGE, groups, LANES), f32),
-            jax.ShapeDtypeStruct((RANGE, groups, LANES), f32),
-            matrices,
-            matrices,
-        ),
-        in_specs=[spec(VMEM)] * 9,
-        out_specs=(spec(VMEM),) * 6,
-        scratch_shapes=[
-            pltpu.VMEM((rows + 2 * RANGE, cols), f32),
-            pltpu.VMEM((4, bands, pixels), f32),
-        ],
-        compiler_params=pltpu.CompilerParams(vmem_limit_bytes=40 << 20),
-        cost_estimate=pl.CostEstimate(flops=10**9, bytes_accessed=16 << 20, transcendentals=0),
-        name="prepare",
-    )(
-        truth_field, truth_above, truth_below, truth_heads, truth_tails, truth_left, truth_right,
-        neighbour_positions, unscaled_neighbour_factor,
-    )
 
     side = jax.ShapeDtypeStruct((groups, members, LANES), f32)
     field, heads, tails = pl.pallas_call(

time: 136 us -> 129 us (0.949)
  blocking collectives: 35.1 us -> 0 us
  waiting for transfers between devices: 0.02 us -> 32.9 us
  Pallas kernels: 76.9 us -> 68.9 us
  local copies, waits for them, and re-layouts: 8.6 us -> 14.4 us
  starting transfers between devices: 13.4 us -> 11.4 us
    all_to_all x1 -> x0, blocking collectives: 35.1 us -> none  [local(): lax.all_to_all(slots, ('face', 'tile'), split_axis=0, concat_axis=0, tile...]
    all_to_all x0 -> x1, waiting for transfers between devices: none -> 30.3 us  [local(): lax.all_to_all(slots, ('face', 'tile'), split_axis=0, concat_axis=0, tile...]
    pallas_call x1 -> x0, Pallas kernels: 8.64 us -> none  [local(): pl.pallas_call(prepare_kernel, out_shape=(jax.ShapeDtypeStruct((2 * RANGE...]
    ppermute x8 -> x4, starting transfers between devices: 13.4 us -> 6.4 us  [shifted(): return lax.ppermute(cells, axis, pairs)]
    unnamed x12 -> x16, local copies, waits for them, and re-layouts: 6.28 us -> 12.7 us
    all_to_all x0 -> x1, starting transfers between devices: none -> 4.96 us  [local(): lax.all_to_all(slots, ('face', 'tile'), split_axis=0, concat_axis=0, tile...]
    ppermute x8 -> x4, waiting for transfers between devices: 0.02 us -> 2.65 us  [shifted(): return lax.ppermute(cells, axis, pairs)]
  transfers between devices with their start and end apart: 8 -> 5, of which waited for: 0 -> 3; matrix products, arithmetic and copies ran while one was open for 1% -> 0% of each run, Pallas kernels for 9% -> 0%
where the time goes in v4:
time: 129 us
  Pallas kernels  68.9 us (53%)
  waiting for transfers between devices  32.9 us (26%)
  local copies, waits for them, and re-layouts  14.4 us (11%)
  starting transfers between devices  11.4 us (9%)
    pallas_call x1, Pallas kernels, local(): pl.pallas_call(functools.partial(fetch_kernel, device_count, tile_count),...  36.7 us
    all_to_all x1, waiting for transfers between devices, local(): lax.all_to_all(slots, ('face', 'tile'), split_axis=0, concat_axis=0, tile...  30.3 us
    pallas_call x1, Pallas kernels, local(): pl.pallas_call(score_kernel, out_shape=jax.ShapeDtypeStruct((device_count...  23.1 us
    unnamed x16, local copies, waits for them, and re-layouts  12.7 us
    ppermute x4, starting transfers between devices, shifted(): return lax.ppermute(cells, axis, pairs)  6.4 us
    pallas_call x1, Pallas kernels, local(): pl.pallas_call(collect_kernel, out_shape=jax.ShapeDtypeStruct((members, b...  5.14 us
    all_to_all x1, starting transfers between devices, local(): lax.all_to_all(slots, ('face', 'tile'), split_axis=0, concat_axis=0, tile...  4.96 us
    pallas_call x1, Pallas kernels, local(): pl.pallas_call(regrid_kernel, out_shape=(jax.ShapeDtypeStruct((bands, mem...  3.97 us
  transfers between devices with their start and end apart: 5, of which 3 were waited for; matrix products, arithmetic and copies ran while one was open for 0% of the time, Pallas kernels for 0%

profile of v4, /device:TPU:0, one launch (start us, length us, event | category | flops | bytes accessed | tf_op | source)
XLA Modules:
  0.0 128.7 jit_solution(2314963713149921794)
XLA Ops:
  0.0 0.7 broadcast_add_fusion.1
  0.7 0.1 copy.15
  0.8 0.1 sub.13
  0.9 0.8 copy.14
  1.7 0.1 reshape.44
  1.8 0.2 convert_reduce_fusion
  2.0 0.1 select_reduce_fusion
  2.2 0.1 add.34
  2.2 0.8 fusion.2
  3.1 0.1 reshape.46.tails
  3.1 0.1 reshape.45.heads
  3.2 1.1 copy.19
  4.4 0.0 copy-start.4
  4.4 0.9 copy-done.4
  5.3 0.0 copy-start.5
  5.3 0.9 copy-done.5
  6.2 0.0 copy-start.6
  6.2 0.8 copy-done.6
  7.0 36.7 %fetch.1 = (bf16[32,8,16,128]{3,2,1,0:T(8,128)(2,1)S(1)}, s32[32,1,128]{2,1,0:T(1,128)S(1)}, f32[16,40,128]{2,1,0:T(8,128)S(1)}, f32[16,32,128]{2,1,0:T(8,128)S(...) custom-call(s32[32,1,128]{2,1,0:T(1,128)S(1)} %pad.4.wanted, ...), custom_call_target="tpu_custom_call" | custom-call | tf_op jit(solution)/shard_map/fetch/pallas_call | solution.py:420
  43.6 0.0 copy-start
  43.7 1.9 %copy-done = bf16[64,128,256]{2,1,0:T(8,128)(2,1)} copy-done((bf16[64,128,256]{2,1,0:T(8,128)(2,1)}, bf16[64,128,256]{2,1,0:T(8,128)(2,1)S(1)}, u32[]{:S(2)}) %copy-start) | copy-done | bytes 4194328
  45.6 0.0 copy-start.2
  45.6 2.0 %copy-done.2 = bf16[64,128,256]{2,1,0:T(8,128)(2,1)} copy-done((bf16[64,128,256]{2,1,0:T(8,128)(2,1)}, bf16[64,128,256]{2,1,0:T(8,128)(2,1)S(1)}, u32[]{:S(2)}) %copy-start.2) | copy-done | bytes 4194328
  47.6 4.0 %regrid.1 = (f32[64,16,128]{2,1,0:T(8,128)S(1)}, f32[2,16,128]{2,1,0:T(8,128)S(1)}, f32[2,16,128]{2,1,0:T(8,128)S(1)}) custom-call(s32[128]{0:T(128)S(1)} %multiply_add_fusion.place, bf16[256,16,128]{2,1,0:T(8,128)(2,1)S(1)} %bitcast.7, s32[4,64,128]{2,1,0:T(8,128)S(1)} %copy-done.4, f32[4,64,128]{2,1,0:T(8,128)S(1)} %copy-done.5), custom_call_target="tpu_custom_call" | custom-call | tf_op jit(solution)/shard_map/regrid/pallas_call | solution.py:465
  51.6 1.3 %collective-permute-start.1 = (f32[16,16,128]{2,1,0:T(8,128)S(1)}, f32[16,16,128]{2,1,0:T(8,128)S(1)}, u32[]{:S(2)}, u32[]{:S(2)}) collective-permute-start(f32[16,16,128]{2,1,0:T(8,128)S(1)} %get-tuple-element.27), channel_id=1, source_target_pairs={{1,0},{2,1},{3,2},{4,3},{5,4},{6,5},{7,6},{9,8},{10,9},{11,10},{12... | collective-permute-start | bytes 393224 | tf_op jit(solution)/shard_map/ppermute | solution.py:385
  52.9 4.6 %collective-permute-start = (f32[16,16,128]{2,1,0:T(8,128)S(1)}, f32[16,16,128]{2,1,0:T(8,128)S(1)}, u32[]{:S(2)}, u32[]{:S(2)}) collective-permute-start(f32[16,16,128]{2,1,0:T(8,128)S(1)} %get-tuple-element.28), channel_id=1, source_target_pairs={{0,1},{1,2},{2,3},{3,4},{4,5},{5,6},{6,7},{8,9},{9,10},{10,11},{11... | collective-permute-start | bytes 393224 | tf_op jit(solution)/shard_map/ppermute | solution.py:385
  57.4 0.1 collective-permute-start.3
  57.5 0.5 collective-permute-start.2
  58.0 0.1 pad_add_fusion.edge
  58.1 0.9 collective-permute-done.3.right_heads
  58.9 1.8 %collective-permute-done.2.left_tails = f32[2,16,128]{2,1,0:T(8,128)S(1)} collective-permute-done((f32[2,16,128]{2,1,0:T(8,128)S(1)}, f32[2,16,128]{2,1,0:T(8,128)S(1)}, u32[]{:S(2)}, u32[]{:S(2)}) %collective-permute-start.2) | collective-permute-done | bytes 16416 | tf_op jit(solution)/shard_map/ppermute | solution.py:385
  60.7 0.0 collective-permute-done.1.below
  60.7 0.0 collective-permute-done.above
  60.7 0.0 copy-start.1
  60.7 2.2 %copy-done.1 = bf16[64,128,256]{2,1,0:T(8,128)(2,1)S(1)} copy-done((bf16[64,128,256]{2,1,0:T(8,128)(2,1)S(1)}, bf16[64,128,256]{2,1,0:T(8,128)(2,1)}, u32[]{:S(2)}) %copy-start.1) | copy-done | bytes 4194328
  62.9 0.0 copy-start.3
  62.9 2.2 %copy-done.3 = bf16[64,128,256]{2,1,0:T(8,128)(2,1)S(1)} copy-done((bf16[64,128,256]{2,1,0:T(8,128)(2,1)S(1)}, bf16[64,128,256]{2,1,0:T(8,128)(2,1)}, u32[]{:S(2)}) %copy-start.3) | copy-done | bytes 4194328
  65.1 23.1 %score.1 = s16[32,9,16,128]{3,2,1,0:T(8,128)(2,1)} custom-call(s32[2]{0:T(128)S(1)} %pad_add_fusion.edge, s32[128]{0:T(128)S(1)} %multiply_add_fusion.place, f32[64,16,128]{2,1,0:T(8,128)S(1)} %get-tuple-element.18.field, f32[16,16,128]{2,1,0:T(8,128)S(1)} %collective-permute-done.above, f32[16,16,128]{2,1,0:T(8,128)S(1)} %collective-permute-done.1.below, ...), custom_call_target="tpu_custom_call" | custom-call | tf_op jit(solution)/shard_map/score/pallas_call | solution.py:485
  88.2 5.0 %all-to-all-start = ((s16[32,9,16,128]{3,2,1,0:T(8,128)(2,1)}), s16[32,9,16,128]{3,2,1,0:T(8,128)(2,1)S(1)}, u32[]{:S(2)}, u32[]{:S(2)}) async-start(s16[32,9,16,128]{3,2,1,0:T(8,128)(2,1)} %score.1), calls=%async_computation | async-start | bytes 2359296 | tf_op jit(solution)/shard_map/all_to_all | solution.py:504
  93.3 0.1 reshape_squeeze.3.wanted
  93.3 30.3 %all-to-all-done.returned = s16[32,9,16,128]{3,2,1,0:T(8,128)(2,1)S(1)} async-done(((s16[32,9,16,128]{3,2,1,0:T(8,128)(2,1)}), s16[32,9,16,128]{3,2,1,0:T(8,128)(2,1)S(1)}, u32[]{:S(2)}, u32[]{:S(2)}) %all-to-all-start) | async-done | bytes 1179680 | tf_op jit(solution)/shard_map/all_to_all | solution.py:504
  123.6 5.1 %collect.1 = f32[16,64,128]{2,1,0:T(8,128)} custom-call(s32[256]{0:T(256)S(1)} %reshape_squeeze.3.wanted, s16[32,9,16,128]{3,2,1,0:T(8,128)(2,1)S(1)} %all-to-all-done.returned), custom_call_target="tpu_custom_call" | custom-call | tf_op jit(solution)/shard_map/collect/pallas_call | solution.py:507
  (5 shorter events, 0.1 us)
Async XLA Ops:
  4.4 0.9 copy-start.4
  5.3 0.9 copy-start.5
  6.2 0.8 copy-start.6
  43.6 1.9 %copy-start = (bf16[64,128,256]{2,1,0:T(8,128)(2,1)}, bf16[64,128,256]{2,1,0:T(8,128)(2,1)S(1)}, u32[]{:S(2)}) copy-start(bf16[64,128,256]{2,1,0:T(8,128)(2,1)S(1)} %get-tuple-element.25.high_far) | copy-start | bytes 12582916
  45.6 2.0 %copy-start.2 = (bf16[64,128,256]{2,1,0:T(8,128)(2,1)}, bf16[64,128,256]{2,1,0:T(8,128)(2,1)S(1)}, u32[]{:S(2)}) copy-start(bf16[64,128,256]{2,1,0:T(8,128)(2,1)S(1)} %get-tuple-element.26.low_far) | copy-start | bytes 12582916
  51.6 9.1 %collective-permute-start.1 = (f32[16,16,128]{2,1,0:T(8,128)S(1)}, f32[16,16,128]{2,1,0:T(8,128)S(1)}, u32[]{:S(2)}, u32[]{:S(2)}) collective-permute-start(f32[16,16,128]{2,1,0:T(8,128)S(1)} %get-tuple-element.27), channel_id=1, source_target_pairs={{1,0},{2,1},{3,2},{4,3},{5,4},{6,5},{7,6},{9,8},{10,9},{11,10},{12... | collective-permute-start | bytes 393224 | tf_op jit(solution)/shard_map/ppermute | solution.py:385
  52.9 7.8 %collective-permute-start = (f32[16,16,128]{2,1,0:T(8,128)S(1)}, f32[16,16,128]{2,1,0:T(8,128)S(1)}, u32[]{:S(2)}, u32[]{:S(2)}) collective-permute-start(f32[16,16,128]{2,1,0:T(8,128)S(1)} %get-tuple-element.28), channel_id=1, source_target_pairs={{0,1},{1,2},{2,3},{3,4},{4,5},{5,6},{6,7},{8,9},{9,10},{10,11},{11... | collective-permute-start | bytes 393224 | tf_op jit(solution)/shard_map/ppermute | solution.py:385
  57.4 1.5 %collective-permute-start.3 = (f32[2,16,128]{2,1,0:T(8,128)S(1)}, f32[2,16,128]{2,1,0:T(8,128)S(1)}, u32[]{:S(2)}, u32[]{:S(2)}) collective-permute-start(f32[2,16,128]{2,1,0:T(8,128)S(1)} %get-tuple-element.19.heads), channel_id=1, source_target_pairs={{8,0},{16,8},{24,16},{0,24},{9,1},{17,9},{25,17},{1,25},{10,2},{18... | collective-permute-start | bytes 49160 | tf_op jit(solution)/shard_map/ppermute | solution.py:385
  57.5 3.2 %collective-permute-start.2 = (f32[2,16,128]{2,1,0:T(8,128)S(1)}, f32[2,16,128]{2,1,0:T(8,128)S(1)}, u32[]{:S(2)}, u32[]{:S(2)}) collective-permute-start(f32[2,16,128]{2,1,0:T(8,128)S(1)} %get-tuple-element.20.tails), channel_id=1, source_target_pairs={{0,8},{8,16},{16,24},{24,0},{1,9},{9,17},{17,25},{25,1},{2,10},{10... | collective-permute-start | bytes 49160 | tf_op jit(solution)/shard_map/ppermute | solution.py:385
  60.7 2.2 %copy-start.1 = (bf16[64,128,256]{2,1,0:T(8,128)(2,1)S(1)}, bf16[64,128,256]{2,1,0:T(8,128)(2,1)}, u32[]{:S(2)}) copy-start(bf16[64,128,256]{2,1,0:T(8,128)(2,1)} %copy-done) | copy-start | bytes 12582916
  62.9 2.2 %copy-start.3 = (bf16[64,128,256]{2,1,0:T(8,128)(2,1)S(1)}, bf16[64,128,256]{2,1,0:T(8,128)(2,1)}, u32[]{:S(2)}) copy-start(bf16[64,128,256]{2,1,0:T(8,128)(2,1)} %copy-done.2) | copy-start | bytes 12582916
  88.2 35.4 %all-to-all-start = ((s16[32,9,16,128]{3,2,1,0:T(8,128)(2,1)}), s16[32,9,16,128]{3,2,1,0:T(8,128)(2,1)S(1)}, u32[]{:S(2)}, u32[]{:S(2)}) async-start(s16[32,9,16,128]{3,2,1,0:T(8,128)(2,1)} %score.1), calls=%async_computation | async-start | bytes 2359296 | tf_op jit(solution)/shard_map/all_to_all | solution.py:504

commit v5 on v4

--- a/solution.py
+++ b/solution.py
@@ -133,6 +133,59 @@
     lax.fori_loop(1, count, got, 0)
     store_high.wait()
     store_low.wait()
+
+
+def sides(count, tiles):
+    faces = count // tiles
+    face, tile = lax.axis_index("face"), lax.axis_index("tile")
+    return (
+        face * tiles + (tile + 1) % tiles,
+        face * tiles + (tile + tiles - 1) % tiles,
+        ((face + 1) % faces) * tiles + tile,
+        ((face + faces - 1) % faces) * tiles + tile,
+    )
+
+
+def halo_kernel(count, tiles, field, heads, tails, above, below, left, right, sent, got):
+    bands, halo = field.shape[0], above.shape[0]
+    others = sides(count, tiles)
+    barrier = pltpu.get_barrier_semaphore()
+    for other in others:
+        pl.semaphore_signal(
+            barrier, inc=1, device_id=place_of(other, tiles), device_id_type=pl.DeviceIdType.MESH
+        )
+    pl.semaphore_wait(barrier, 4)
+    copies = []
+    for i, (source, target) in enumerate((
+        (field.at[pl.ds(bands - halo, halo)], above),
+        (field.at[pl.ds(0, halo)], below),
+        (tails, left),
+        (heads, right),
+    )):
+        copies.append(remote(source, target, sent.at[i], got.at[i], others[i], tiles))
+    for copy in copies:
+        copy.start()
+    for copy in copies:
+        copy.wait()
+
+
+def return_kernel(count, tiles, slots, returned, sent, got):
+    me = lax.axis_index("face") * tiles + lax.axis_index("tile")
+    greet(count, tiles, me)
+
+    def send(s, carry):
+        other = (me + s) % count
+        remote(slots.at[other], returned.at[me], sent.at[s], got.at[s], other, tiles).start()
+        return carry
+
+    def wait(s, carry):
+        other = (me + s) % count
+        remote(slots.at[other], returned.at[me], sent.at[s], got.at[s], other, tiles).wait()
+        return carry
+
+    lax.fori_loop(1, count, send, 0)
+    returned[me] = slots[me]
+    lax.fori_loop(1, count, wait, 0)
 
 
 def regrid_kernel(place, incoming, positions, factors, field, heads, tails, weights):
@@ -370,19 +423,6 @@
     lax.fori_loop(0, returned.shape[0], step, 0, unroll=4)
     for g in range(bands):
         slope[:, g, :] = summed[g]
-
-
-def halves(planes):
-    return jnp.stack([p[:, at : at + LANES] for p in planes for at in (0, LANES)])
-
-
-def shifted(cells, axis, step, closed):
-    count = lax.axis_size(axis)
-    ends = count if closed else count - 1
-    pairs = [(i, (i + 1) % count) for i in range(ends)]
-    if step < 0:
-        pairs = [(b, a) for a, b in pairs]
-    return lax.ppermute(cells, axis, pairs)
 
 
 def local(
@@ -451,7 +491,7 @@
             pltpu.SemaphoreType.DMA((2,)),
         ],
         compiler_params=pltpu.CompilerParams(
-            collective_id=1, has_side_effects=True, vmem_limit_bytes=40 << 20
+            collective_id=1, has_side_effects=True, vmem_limit_bytes=56 << 20
         ),
         name="fetch",
     )(
@@ -468,15 +508,23 @@
         in_specs=[spec(SMEM), spec(VMEM), spec(VMEM), spec(VMEM)],
         out_specs=(spec(VMEM), spec(VMEM), spec(VMEM)),
         scratch_shapes=[pltpu.VMEM((4, bands, pixels), f32)],
-        compiler_params=pltpu.CompilerParams(vmem_limit_bytes=32 << 20),
+        compiler_params=pltpu.CompilerParams(vmem_limit_bytes=56 << 20),
         name="regrid",
     )(place, incoming, neighbour_positions, unscaled_neighbour_factor)
 
     halo = 2 * RANGE
-    above = shifted(field[bands - halo :], "tile", 1, False)
-    below = shifted(field[:halo], "tile", -1, False)
-    left_tails = shifted(tails, "face", 1, True)
-    right_heads = shifted(heads, "face", -1, True)
+    strip_halo = jax.ShapeDtypeStruct((halo, members, pixels), f32)
+    above, below, left_tails, right_heads = pl.pallas_call(
+        functools.partial(halo_kernel, device_count, tile_count),
+        out_shape=(strip_halo, strip_halo, side, side),
+        in_specs=[spec(VMEM)] * 3,
+        out_specs=(spec(VMEM),) * 4,
+        scratch_shapes=[pltpu.SemaphoreType.DMA((4,)), pltpu.SemaphoreType.DMA((4,))],
+        compiler_params=pltpu.CompilerParams(
+            collective_id=2, has_side_effects=True, vmem_limit_bytes=56 << 20
+        ),
+        name="halo",
+    )(field, heads, tails)
     tile = lax.axis_index("tile")
     edge = jnp.stack(
         [RANGE - tile * rows, RANGE + (tile_count - tile) * rows]
@@ -495,22 +543,33 @@
             pltpu.VMEM((bands, pixels, 2 * pixels), jnp.bfloat16),
             pltpu.SemaphoreType.DMA((2,)),
         ],
-        compiler_params=pltpu.CompilerParams(vmem_limit_bytes=40 << 20),
+        compiler_params=pltpu.CompilerParams(vmem_limit_bytes=56 << 20),
         name="score",
     )(
         edge, place, field, above, below, heads, tails, left_tails, right_heads,
         root_tall, root_wide, root_left, root_right, high, low,
     )
-    returned = lax.all_to_all(
-        slots, ("face", "tile"), split_axis=0, concat_axis=0, tiled=True
-    )
+    returned = pl.pallas_call(
+        functools.partial(return_kernel, device_count, tile_count),
+        out_shape=jax.ShapeDtypeStruct(slots.shape, slots.dtype),
+        in_specs=[spec(VMEM)],
+        out_specs=spec(VMEM),
+        scratch_shapes=[
+            pltpu.SemaphoreType.DMA((device_count,)),
+            pltpu.SemaphoreType.DMA((device_count,)),
+        ],
+        compiler_params=pltpu.CompilerParams(
+            collective_id=3, has_side_effects=True, vmem_limit_bytes=56 << 20
+        ),
+        name="give_back",
+    )(slots)
     return pl.pallas_call(
         collect_kernel,
         out_shape=jax.ShapeDtypeStruct((members, bands, pixels), f32),
         in_specs=[spec(SMEM), spec(VMEM)],
         out_specs=spec(VMEM),
         scratch_shapes=[pltpu.VMEM((bands + 8, members, pixels), f32)],
-        compiler_params=pltpu.CompilerParams(vmem_limit_bytes=32 << 20),
+        compiler_params=pltpu.CompilerParams(vmem_limit_bytes=56 << 20),
         name="collect",
     )(asked, returned)
 

time: 129 us -> 126 us (0.977)
  Pallas kernels: 68.9 us -> 117 us
  waiting for transfers between devices: 32.9 us -> 0 us
  starting transfers between devices: 11.4 us -> 0 us
  local copies, waits for them, and re-layouts: 14.4 us -> 7.25 us
    pallas_call x0 -> x2, Pallas kernels: none -> 42.7 us  [the longest x1 31.7 us: local(): pl.pallas_call(functools.partial(return_kernel, device_count, tile_count)...]
    all_to_all x1 -> x0, waiting for transfers between devices: 30.3 us -> none  [local(): lax.all_to_all(slots, ('face', 'tile'), split_axis=0, concat_axis=0, tile...]
    unnamed x16 -> x4, local copies, waits for them, and re-layouts: 12.7 us -> 2.6 us
    ppermute x4 -> x0, starting transfers between devices: 6.4 us -> none  [shifted(): return lax.ppermute(cells, axis, pairs)]
    all_to_all x1 -> x0, starting transfers between devices: 4.96 us -> none  [local(): lax.all_to_all(slots, ('face', 'tile'), split_axis=0, concat_axis=0, tile...]
    ppermute x4 -> x0, waiting for transfers between devices: 2.65 us -> none  [shifted(): return lax.ppermute(cells, axis, pairs)]
    pallas_call x1, Pallas kernels: 36.7 us -> 39 us  [local(): pl.pallas_call(functools.partial(fetch_kernel, device_count, tile_count),...]
    pallas_call x1, Pallas kernels: 3.97 us -> 5.47 us  [local(): pl.pallas_call(regrid_kernel, out_shape=(jax.ShapeDtypeStruct((bands, mem...]
  transfers between devices with their start and end apart: 5 -> 0, of which waited for: 3 -> 0; matrix products, arithmetic and copies ran while one was open for 0% -> 0% of each run, Pallas kernels for 0% -> 0%
where the time goes in v5:
time: 126 us; the launch traced here: 125 us
  Pallas kernels  117 us (93%)
  local copies, waits for them, and re-layouts  7.25 us (6%)
  other arithmetic  1.6 us (1%)
    pallas_call x1, Pallas kernels, local(): pl.pallas_call(functools.partial(fetch_kernel, device_count, tile_count),...  39 us
    pallas_call x1, Pallas kernels, local(): pl.pallas_call(functools.partial(return_kernel, device_count, tile_count)...  31.7 us
    pallas_call x1, Pallas kernels, local(): pl.pallas_call(score_kernel, out_shape=jax.ShapeDtypeStruct((device_count...  23.5 us
    pallas_call x1, Pallas kernels, local(): pl.pallas_call(functools.partial(halo_kernel, device_count, tile_count),...  11 us
    pallas_call x1, Pallas kernels, local(): pl.pallas_call(collect_kernel, out_shape=jax.ShapeDtypeStruct((members, b...  5.89 us
    pallas_call x1, Pallas kernels, local(): pl.pallas_call(regrid_kernel, out_shape=(jax.ShapeDtypeStruct((bands, mem...  5.47 us
    unnamed x4, local copies, waits for them, and re-layouts  2.6 us

profile of v5, /device:TPU:0, one launch (start us, length us, event | category | flops | bytes accessed | tf_op | source)
XLA Modules:
  0.0 125.5 jit_solution(6006974384053268878)
XLA Ops:
  0.0 0.6 pad_add_fusion.edge
  0.6 0.7 broadcast_add_fusion.1
  1.3 0.1 copy.15
  1.4 0.1 sub.13
  1.5 0.8 copy.14
  2.3 0.1 reshape.44
  2.4 0.2 convert_reduce_fusion
  2.6 0.0 copy-start
  2.7 0.1 select_reduce_fusion
  2.8 0.1 add.34
  2.9 0.6 pad.4.wanted
  3.5 0.8 fusion.1
  4.3 0.7 reshape.46.tails
  5.0 0.7 reshape.45.heads
  5.6 1.8 %copy.19 = bf16[16,64,128]{2,0,1:T(8,128)(2,1)} copy(bf16[16,64,128]{2,1,0:T(8,128)(2,1)} %param.6) | data formatting | bytes 524288 | tf_op args[0]
  7.5 39.0 %fetch.1 = (bf16[32,8,16,128]{3,2,1,0:T(8,128)(2,1)}, s32[32,1,128]{2,1,0:T(1,128)}, f32[16,40,128]{2,1,0:T(8,128)}, f32[16,32,128]{2,1,0:T(8,128)}, f32[8,2,128...) custom-call(s32[32,1,128]{2,1,0:T(1,128)} %pad.4.wanted, ...), custom_call_target="tpu_custom_call" | custom-call | tf_op jit(solution)/shard_map/fetch/pallas_call | solution.py:460
  46.5 0.8 slice_reduce_fusion
  47.2 0.7 reshape_squeeze.3.wanted
  47.9 0.0 copy-done
  47.9 5.5 %regrid.1 = (f32[64,16,128]{2,1,0:T(8,128)}, f32[2,16,128]{2,1,0:T(8,128)}, f32[2,16,128]{2,1,0:T(8,128)}) custom-call(s32[128]{0:T(128)} %copy-done, bf16[256,16,128]{2,1,0:T(8,128)(2,1)} %bitcast.7, s32[4,64,128]{2,1,0:T(8,128)} %positions.3, f32[4,64,128]{2,1,0:T(8,128)} %factors.3), custom_call_target="tpu_custom_call" | custom-call | tf_op jit(solution)/shard_map/regrid/pallas_call | solution.py:505
  53.4 11.0 %halo.1 = (f32[16,16,128]{2,1,0:T(8,128)}, f32[16,16,128]{2,1,0:T(8,128)}, f32[2,16,128]{2,1,0:T(8,128)}, f32[2,16,128]{2,1,0:T(8,128)}) custom-call(f32[64,16,128]{2,1,0:T(8,128)} %get-tuple-element.22.field, f32[2,16,128]{2,1,0:T(8,128)} %get-tuple-element.23.heads, f32[2,16,128]{2,1,0:T(8,128)} %get-tuple-element.24.tails), custom_call_target="tpu_custom_call" | custom-call | tf_op jit(solution)/shard_map/halo/pallas_call | solution.py:517
  64.3 23.5 %score.1.slots = s16[32,9,16,128]{3,2,1,0:T(8,128)(2,1)} custom-call(s32[2]{0:T(128)} %pad_add_fusion.edge, s32[128]{0:T(128)} %copy-done, f32[64,16,128]{2,1,0:T(8,128)} %get-tuple-element.22.field, f32[16,16,128]{2,1,0:T(8,128)} %get-tuple-element.25.above, f32[16,16,128]{2,1,0:T(8,128)} %get-tuple-element.26.below, ...), custom_call_target="tpu_custom_call" | custom-call | tf_op jit(solution)/shard_map/score/pallas_call | solution.py:533
  87.8 31.7 %give_back.1.returned = s16[32,9,16,128]{3,2,1,0:T(8,128)(2,1)} custom-call(s16[32,9,16,128]{3,2,1,0:T(8,128)(2,1)} %score.1.slots), custom_call_target="tpu_custom_call" | custom-call | tf_op jit(solution)/shard_map/give_back/pallas_call | solution.py:552
  119.6 5.9 %collect.1 = f32[16,64,128]{2,1,0:T(8,128)} custom-call(s32[256]{0:T(256)} %reshape_squeeze.3.wanted, s16[32,9,16,128]{3,2,1,0:T(8,128)(2,1)} %give_back.1.returned), custom_call_target="tpu_custom_call" | custom-call | tf_op jit(solution)/shard_map/collect/pallas_call | solution.py:566
  (2 shorter events, 0.0 us)
Async XLA Ops:
  2.6 45.2 %copy-start = (s32[128]{0:T(128)}, s32[128]{0:T(128)S(1)}, u32[]{:S(2)}) copy-start(s32[128]{0:T(128)S(1)} %multiply_add_fusion.place) | copy-start | bytes 1540

commit v6 on v5

--- a/solution.py
+++ b/solution.py
@@ -163,10 +163,27 @@
         (heads, right),
     )):
         copies.append(remote(source, target, sent.at[i], got.at[i], others[i], tiles))
-    for copy in copies:
-        copy.start()
-    for copy in copies:
-        copy.wait()
+    tile = lax.axis_index("tile")
+    first, last = tile == 0, tile == tiles - 1
+    pl.when(jnp.logical_not(last))(copies[0].start)
+    pl.when(jnp.logical_not(first))(copies[1].start)
+    copies[2].start()
+    copies[3].start()
+
+    @pl.when(first)
+    def _():
+        above[...] = jnp.zeros_like(above)
+
+    @pl.when(last)
+    def _():
+        below[...] = jnp.zeros_like(below)
+
+    pl.when(jnp.logical_not(last))(copies[0].wait_send)
+    pl.when(jnp.logical_not(first))(copies[0].wait_recv)
+    pl.when(jnp.logical_not(first))(copies[1].wait_send)
+    pl.when(jnp.logical_not(last))(copies[1].wait_recv)
+    copies[2].wait()
+    copies[3].wait()
 
 
 def return_kernel(count, tiles, slots, returned, sent, got):
@@ -399,7 +416,7 @@
 
     fetch_high.wait()
     fetch_low.wait()
-    lax.fori_loop(0, rows, wide_step, 0)
+    lax.fori_loop(0, rows, wide_step, 0, unroll=2)
     for holder in range(slots.shape[0]):
         slots[holder, slot_count] = scales[holder].astype(jnp.int16)
 

time: 126 us -> 120 us (0.952)
  Pallas kernels: 117 us -> 110 us
    pallas_call x1, Pallas kernels: 23.5 us -> 17.4 us  [local(): pl.pallas_call(score_kernel, out_shape=jax.ShapeDtypeStruct((device_count...]
where the time goes in v6:
time: 120 us; the launch traced here: 119 us
  Pallas kernels  110 us (92%)
  local copies, waits for them, and re-layouts  7.25 us (6%)
  other arithmetic  1.6 us (1%)
    pallas_call x1, Pallas kernels, local(): pl.pallas_call(functools.partial(fetch_kernel, device_count, tile_count),...  39 us
    pallas_call x1, Pallas kernels, local(): pl.pallas_call(functools.partial(return_kernel, device_count, tile_count)...  32.4 us
    pallas_call x1, Pallas kernels, local(): pl.pallas_call(score_kernel, out_shape=jax.ShapeDtypeStruct((device_count...  17.4 us
    pallas_call x1, Pallas kernels, local(): pl.pallas_call(functools.partial(halo_kernel, device_count, tile_count),...  10.3 us
    pallas_call x1, Pallas kernels, local(): pl.pallas_call(collect_kernel, out_shape=jax.ShapeDtypeStruct((members, b...  5.81 us
    pallas_call x1, Pallas kernels, local(): pl.pallas_call(regrid_kernel, out_shape=(jax.ShapeDtypeStruct((bands, mem...  5.47 us
    unnamed x4, local copies, waits for them, and re-layouts  2.6 us

profile of v6, /device:TPU:0, one launch (start us, length us, event | category | flops | bytes accessed | tf_op | source)
XLA Modules:
  0.0 119.3 jit_solution(12209994591332762554)
XLA Ops:
  0.0 0.6 pad_add_fusion.edge
  0.6 0.7 broadcast_add_fusion.1
  1.3 0.1 copy.15
  1.4 0.1 sub.13
  1.5 0.8 copy.14
  2.3 0.1 reshape.44
  2.4 0.2 convert_reduce_fusion
  2.6 0.0 copy-start
  2.7 0.1 select_reduce_fusion
  2.8 0.1 add.34
  2.9 0.6 pad.4.wanted
  3.5 0.8 fusion.1
  4.3 0.7 reshape.46.tails
  5.0 0.7 reshape.45.heads
  5.6 1.8 %copy.19 = bf16[16,64,128]{2,0,1:T(8,128)(2,1)} copy(bf16[16,64,128]{2,1,0:T(8,128)(2,1)} %param.6) | data formatting | bytes 524288 | tf_op args[0]
  7.5 39.0 %fetch.1 = (bf16[32,8,16,128]{3,2,1,0:T(8,128)(2,1)}, s32[32,1,128]{2,1,0:T(1,128)}, f32[16,40,128]{2,1,0:T(8,128)}, f32[16,32,128]{2,1,0:T(8,128)}, f32[8,2,128...) custom-call(s32[32,1,128]{2,1,0:T(1,128)} %pad.4.wanted, ...), custom_call_target="tpu_custom_call" | custom-call | tf_op jit(solution)/shard_map/fetch/pallas_call | solution.py:477
  46.5 0.8 slice_reduce_fusion
  47.2 0.7 reshape_squeeze.3.wanted
  47.9 0.0 copy-done
  47.9 5.5 %regrid.1 = (f32[64,16,128]{2,1,0:T(8,128)}, f32[2,16,128]{2,1,0:T(8,128)}, f32[2,16,128]{2,1,0:T(8,128)}) custom-call(s32[128]{0:T(128)} %copy-done, bf16[256,16,128]{2,1,0:T(8,128)(2,1)} %bitcast.7, s32[4,64,128]{2,1,0:T(8,128)} %positions.3, f32[4,64,128]{2,1,0:T(8,128)} %factors.3), custom_call_target="tpu_custom_call" | custom-call | tf_op jit(solution)/shard_map/regrid/pallas_call | solution.py:522
  53.4 10.3 %halo.1 = (f32[16,16,128]{2,1,0:T(8,128)}, f32[16,16,128]{2,1,0:T(8,128)}, f32[2,16,128]{2,1,0:T(8,128)}, f32[2,16,128]{2,1,0:T(8,128)}) custom-call(f32[64,16,128]{2,1,0:T(8,128)} %get-tuple-element.22.field, f32[2,16,128]{2,1,0:T(8,128)} %get-tuple-element.23.heads, f32[2,16,128]{2,1,0:T(8,128)} %get-tuple-element.24.tails), custom_call_target="tpu_custom_call" | custom-call | tf_op jit(solution)/shard_map/halo/pallas_call | solution.py:534
  63.7 17.4 %score.1.slots = s16[32,9,16,128]{3,2,1,0:T(8,128)(2,1)} custom-call(s32[2]{0:T(128)} %pad_add_fusion.edge, s32[128]{0:T(128)} %copy-done, f32[64,16,128]{2,1,0:T(8,128)} %get-tuple-element.22.field, f32[16,16,128]{2,1,0:T(8,128)} %get-tuple-element.25.above, f32[16,16,128]{2,1,0:T(8,128)} %get-tuple-element.26.below, ...), custom_call_target="tpu_custom_call" | custom-call | tf_op jit(solution)/shard_map/score/pallas_call | solution.py:550
  81.1 32.4 %give_back.1.returned = s16[32,9,16,128]{3,2,1,0:T(8,128)(2,1)} custom-call(s16[32,9,16,128]{3,2,1,0:T(8,128)(2,1)} %score.1.slots), custom_call_target="tpu_custom_call" | custom-call | tf_op jit(solution)/shard_map/give_back/pallas_call | solution.py:569
  113.5 5.8 %collect.1 = f32[16,64,128]{2,1,0:T(8,128)} custom-call(s32[256]{0:T(256)} %reshape_squeeze.3.wanted, s16[32,9,16,128]{3,2,1,0:T(8,128)(2,1)} %give_back.1.returned), custom_call_target="tpu_custom_call" | custom-call | tf_op jit(solution)/shard_map/collect/pallas_call | solution.py:583
  (2 shorter events, 0.0 us)
Async XLA Ops:
  2.6 45.2 %copy-start = (s32[128]{0:T(128)}, s32[128]{0:T(128)S(1)}, u32[]{:S(2)}) copy-start(s32[128]{0:T(128)S(1)} %multiply_add_fusion.place) | copy-start | bytes 1540
